TPU v7x, 32 devices: a whole 2x2x4 slice. The times are simulated.
32 devices in a mesh: groups: 2 (over x), dp: 8 (over z, y), mp: 2 (over core).
Axes of the slice: x: 2, y: 2, z: 4, core: 2. Of those that a mesh axis runs over, the one named last changes fastest.
Arguments:
- prompt_hidden: bfloat16 [32, 256, 5120], P(('groups', 'dp')), parts along dimension 0, may hold values from -6 to 6
- completion_hidden: bfloat16 [128, 64, 5120], P(('groups', 'dp')), parts along dimension 0, may hold values from -6 to 6
- queries: bfloat16 [128, 64, 4096], P(('groups', 'dp'), None, 'mp'), parts along dimension 0, may hold values from -72 to 72
- cotangent: bfloat16 [128, 64, 4096], P(('groups', 'dp'), None, 'mp'), parts along dimension 0, may hold values from -6 to 6
- kv_weight: bfloat16 [5120, 2, 512], P('dp', None, 'mp'), may hold values from -0.078125 to 0.078125
- prompt_of: int32 [128], P(('groups', 'dp')), parts along dimension 0, may hold values from 0 to 15, as said below
- comp_len: int32 [16, 8], P(('groups', 'dp')), parts along dimension 0, may hold values from 1 to 64, 384 in all within a row
Outputs:
- attended: bfloat16 [128, 64, 4096], P(('groups', 'dp'), None, 'mp'), parts along dimension 0
- grad_queries: bfloat16 [128, 64, 4096], P(('groups', 'dp'), None, 'mp'), parts along dimension 0
- grad_prompt_hidden: bfloat16 [32, 256, 5120], P(('groups', 'dp'), None, 'mp'), parts along dimension 0
- grad_completion_hidden: bfloat16 [128, 64, 5120], P(('groups', 'dp'), None, 'mp'), parts along dimension 0
- grad_kv_weight: float32 [10240, 2, 512], P(('groups', 'dp'), None, 'mp'), parts along dimension 0
There are 2 independent parts, one for each index of `groups`. A program takes and returns all parts, laid end to end along the dimension named above; an argument that names none is the same for every part. Nothing has to cross between parts.
Inputs may be any that keep to these rules, and one draw needn't show every extreme that they name: `prompt_of`: prompt p is held by index p // 2 of dp. The 8 completions held by one index of dp continue prompts of 8 different holders.
All inputs are finite; a program needn't handle non-finite values.
Results may differ from a plain program's by a relative error of at most 0.02.
The roundings to bfloat16 on the way count: a program that leaves them out, or rounds other values in their place, can miss the bound.
Values may be sent and summed in bfloat16 or wider, within the bound.
A program may use at most 192 MiB of HBM per device.

v0:
```python
import jax
import jax.numpy as jnp
from jax import lax
from jax.sharding import PartitionSpec as P

HEAD_DIM = 128


def shards(prompt_hidden, completion_hidden, queries, cotangent, kv_weight, prompt_of, comp_len):
    weights_all = lax.all_gather(kv_weight, "dp", axis=0, tiled=True)
    model_dim = weights_all.shape[0]
    kv_width = weights_all.shape[2]
    flat_weights = weights_all.reshape(model_dim, 2 * kv_width)
    prompt_count, prompt_len = (prompt_hidden.shape[0], prompt_hidden.shape[1])
    comp_count, comp_length = (completion_hidden.shape[0], completion_hidden.shape[1])
    prompt_flat = prompt_hidden.reshape(prompt_count * prompt_len, model_dim)
    own_flat = completion_hidden.reshape(comp_count * comp_length, model_dim)
    prompt_kv = (
        jnp.dot(prompt_flat, flat_weights, preferred_element_type=jnp.float32)
        .astype(jnp.bfloat16)
        .reshape(prompt_count, prompt_len, 2, kv_width)
    )
    own_kv = (
        jnp.dot(own_flat, flat_weights, preferred_element_type=jnp.float32)
        .astype(jnp.bfloat16)
        .reshape(comp_count, comp_length, 2, kv_width)
    )
    holders = lax.axis_size("dp")
    everything = lax.all_gather(prompt_kv, "dp", axis=0, tiled=True)
    chosen = everything[prompt_of]
    kv_here = kv_width // HEAD_DIM
    heads_here = queries.shape[2] // HEAD_DIM
    group_size = heads_here // kv_here
    score_scale = HEAD_DIM ** (-0.5)
    total_keys = prompt_len + comp_length
    key_rows = jnp.concatenate([chosen[:, :, 0], own_kv[:, :, 0]], axis=1).reshape(
        comp_count, total_keys, kv_here, HEAD_DIM
    )
    value_rows = jnp.concatenate([chosen[:, :, 1], own_kv[:, :, 1]], axis=1).reshape(
        comp_count, total_keys, kv_here, HEAD_DIM
    )
    query_blocks = queries.reshape(comp_count, comp_length, kv_here, group_size, HEAD_DIM)
    scores = (
        jnp.einsum("cikgd,cjkd->ckgij", query_blocks, key_rows, preferred_element_type=jnp.float32)
        * score_scale
    )
    row_ids = jnp.arange(comp_length, dtype=jnp.int32)[:, None]
    col_ids = jnp.arange(total_keys, dtype=jnp.int32)[None, :]
    allowed = (col_ids < prompt_len) | (col_ids - prompt_len <= row_ids)
    scores = jnp.where(allowed, scores, -1e30)
    row_max = jnp.max(scores, axis=-1, keepdims=True)
    expo_scores = jnp.exp(scores - row_max)
    probabilities = expo_scores / jnp.sum(expo_scores, axis=-1, keepdims=True)
    weights = probabilities.astype(jnp.bfloat16)
    live_rows = (jnp.arange(comp_length, dtype=jnp.int32)[None, :] < comp_len.reshape(-1)[:, None])[
        :, :, None, None, None
    ]
    mixed_out = jnp.einsum(
        "ckgij,cjkd->cikgd", weights, value_rows, preferred_element_type=jnp.float32
    )
    attended = (
        jnp.where(live_rows, mixed_out, 0.0)
        .astype(jnp.bfloat16)
        .reshape(comp_count, comp_length, -1)
    )
    live_cot = jnp.where(
        live_rows,
        cotangent.reshape(comp_count, comp_length, kv_here, group_size, HEAD_DIM),
        jnp.zeros((), jnp.bfloat16),
    )
    prob_grad = jnp.einsum(
        "cikgd,cjkd->ckgij", live_cot, value_rows, preferred_element_type=jnp.float32
    )
    row_delta = jnp.sum(probabilities * prob_grad, axis=-1, keepdims=True)
    score_grad = (probabilities * (prob_grad - row_delta) * score_scale).astype(jnp.bfloat16)
    grad_queries = (
        jnp.einsum("ckgij,cjkd->cikgd", score_grad, key_rows, preferred_element_type=jnp.float32)
        .astype(jnp.bfloat16)
        .reshape(comp_count, comp_length, -1)
    )
    key_grads = jnp.einsum(
        "ckgij,cikgd->cjkd", score_grad, query_blocks, preferred_element_type=jnp.float32
    ).reshape(comp_count, total_keys, kv_width)
    value_grads = jnp.einsum(
        "ckgij,cikgd->cjkd", weights, live_cot, preferred_element_type=jnp.float32
    ).reshape(comp_count, total_keys, kv_width)
    kv_grads = jnp.stack([key_grads, value_grads], axis=2)
    prompt_terms = kv_grads[:, :prompt_len].astype(jnp.bfloat16)
    own_grads = kv_grads[:, prompt_len:].astype(jnp.bfloat16)
    row_index = jnp.arange(lax.axis_size("dp") * prompt_count, dtype=jnp.int32)
    row_hit = (row_index[:, None] == prompt_of[None, :]).astype(jnp.bfloat16)
    prompt_sum = lax.psum_scatter(
        jnp.einsum(
            "pc,clkw->plkw", row_hit, prompt_terms, preferred_element_type=jnp.float32
        ).astype(jnp.bfloat16),
        "dp",
        scatter_dimension=0,
        tiled=True,
    )
    prompt_grad_flat = prompt_sum.reshape(prompt_count * prompt_len, 2 * kv_width)
    own_grad_flat = own_grads.reshape(comp_count * comp_length, 2 * kv_width)
    contract_last = (((1,), (1,)), ((), ()))
    prompt_part = lax.dot_general(
        prompt_grad_flat, flat_weights, contract_last, preferred_element_type=jnp.float32
    )
    own_part = lax.dot_general(
        own_grad_flat, flat_weights, contract_last, preferred_element_type=jnp.float32
    )
    prompt_part = (
        lax.optimization_barrier(prompt_part.astype(jnp.bfloat16))
        .astype(jnp.float32)
        .reshape(prompt_count, prompt_len, model_dim)
    )
    own_part = (
        lax.optimization_barrier(own_part.astype(jnp.bfloat16))
        .astype(jnp.float32)
        .reshape(comp_count, comp_length, model_dim)
    )
    prompt_feat, own_feat = (
        lax.psum_scatter(
            prompt_part.astype(jnp.bfloat16), "mp", scatter_dimension=2, tiled=True
        ).astype(jnp.float32),
        lax.psum_scatter(
            own_part.astype(jnp.bfloat16), "mp", scatter_dimension=2, tiled=True
        ).astype(jnp.float32),
    )
    contract_first = (((0,), (0,)), ((), ()))
    prompt_term = lax.dot_general(
        prompt_flat, prompt_grad_flat, contract_first, preferred_element_type=jnp.float32
    )
    own_term = lax.dot_general(
        own_flat, own_grad_flat, contract_first, preferred_element_type=jnp.float32
    )
    grad_kv_weight = lax.psum_scatter(
        (prompt_term + own_term).reshape(model_dim // holders * lax.axis_size("dp"), 2, kv_width),
        "dp",
        scatter_dimension=0,
        tiled=True,
    )
    return (
        attended,
        grad_queries,
        prompt_feat.astype(jnp.bfloat16),
        own_feat.astype(jnp.bfloat16),
        grad_kv_weight,
    )


def solution(mesh):
    in_specs = (
        P(("groups", "dp"), None, None),
        P(("groups", "dp"), None, None),
        P(("groups", "dp"), None, "mp"),
        P(("groups", "dp"), None, "mp"),
        P("dp", None, "mp"),
        P(("groups", "dp")),
        P(("groups", "dp"), None),
    )
    out_specs = (
        P(("groups", "dp"), None, "mp"),
        P(("groups", "dp"), None, "mp"),
        P(("groups", "dp"), None, "mp"),
        P(("groups", "dp"), None, "mp"),
        P(("groups", "dp"), None, "mp"),
    )
    return jax.shard_map(shards, mesh=mesh, in_specs=in_specs, out_specs=out_specs, check_vma=False)
```

profile of v0, /device:TPU:0, one launch (start us, length us, event | category | flops | bytes accessed | tf_op | source)
XLA Modules:
  0.0 779.1 jit_solution(10103510933410721781)
XLA Ops:
  7.9 91.2 %all-gather.3.cloned.1.call-done = bf16[5120,2,256]{2,1,0:T(2,128)(2,1)} async-done(((bf16[640,2,256]{2,1,0:T(2,128)(2,1)}), bf16[5120,2,256]{2,1,0:T(2,128)(2,1)}) %all-gather.3.cloned.1.call-update) | async-done | bytes 5242896 | tf_op jit(solution)/shard_map/all_gather | solution.py:10
  99.2 3.5 copy.90
  105.0 2.9 convolution_convert_fusion.4
  111.2 3.5 copy.92
  114.9 7.1 convolution_convert_fusion.3
  125.2 55.4 %all-gather.5.cloned.1.call-done = bf16[16,256,2,256]{3,1,2,0:T(8,128)(2,1)} async-done(((bf16[2,256,2,256]{3,1,2,0:T(8,128)(2,1)}), bf16[16,256,2,256]{3,1,2,0:T(8,128)(2,1)}) %all-gather.5.cloned.1.call-update) | async-done | bytes 4194320 | tf_op jit(solution)/shard_map/all_gather | solution.py:29
  180.7 4.2 gather_fusion
  184.8 3.0 fusion.48
  193.6 3.0 fusion.19
  196.6 7.7 fusion.49
  204.3 7.3 fusion.24
  211.7 2.4 copy.83
  214.1 3.8 reshape.125
  217.8 8.3 %fusion.29 = f32[8,2,320,64,8]{2,3,4,1,0:T(8,128)} fusion(bf16[8,64,2,8,128]{4,3,2,1,0:T(8,128)(2,1)} %bitcast.137, pred[8,64]{1,0:T(8,128)(4,1)S(1)} %iota_compare_fusion.2, bf16[8,64,2,128]{3,1,2,0:T(8,128)(2,1)} %copy_bitcast_fusion.1, bf16[8,256,2,128]{3,1,2,0:T(8,128)(2,1)} %copy.58), kind=kOutput, calls=%fused_computation.37 | convolution fusion | flops 674758656 | bytes 13894144 | tf_op jit(solution)/shard_map/cikgd,cjkd->ckgij/dot_general | solution.py:71
  226.2 57.9 %fusion.21 = bf16[8,320,2,128]{3,1,2,0:T(8,128)(2,1)} fusion(bf16[8,64,2,8,128]{4,3,2,1,0:T(8,128)(2,1)S(1)} %bitcast.135, f32[8,2,320,64,8]{2,3,4,1,0:T(8,128)} %fusion.29, f32[8,2,8,64,320]{4,3,2,1,0:T(8,128)} %get-tuple-element.10, f32[8,2,8,64]{3,2,1,0:T(8,128)S(1)} %get-tuple-element.9), kind=kOutput, calls=%fused_computation.35 | convolution fusion | flops 689447232 | bytes 24412160 | tf_op jit(solution)/shard_map/ckgij,cikgd->cjkd/dot_general | solution.py:81
  284.0 3.7 copy.82
  287.8 3.4 reshape.124
  293.1 4.4 copy.73
  298.3 85.5 %reduce-scatter.4.cloned.1.call-done = bf16[2,256,2,256]{3,1,2,0:T(8,128)(2,1)} async-done(((bf16[16,256,2,256]{3,1,2,0:T(8,128)(2,1)}), bf16[2,256,2,256]{3,1,2,0:T(8,128)(2,1)}) %reduce-scatter.4.cloned.1.call-update) | async-done | bytes 524304 | tf_op jit(solution)/shard_map/reduce_scatter | solution.py:92
  385.5 5.1 fusion.50
  390.6 5.8 convolution_add_fusion
  396.4 16.1 %copy.76 = f32[5120,2,256]{2,1,0:T(2,128)} copy(f32[5120,2,256]{0,2,1:T(8,128)} %bitcast.129) | data formatting | bytes 20971520 | tf_op jit(solution)/shard_map/reshape | solution.py:135
  412.5 7.1 convolution_convert_fusion
  419.7 7.1 convolution_convert_fusion.1
  428.7 5.8 fusion.16
  438.3 54.7 %convert_bitcast_fusion = bf16[8,64,2,8,128]{4,1,3,2,0:T(8,128)(2,1)} fusion(f32[8,2,320,64,8]{2,3,4,1,0:T(8,128)} %fusion.29, bf16[8,64,2,128]{3,1,2,0:T(8,128)(2,1)S(1)} %copy-done.4, bf16[8,256,2,128]{3,1,2,0:T(8,128)(2,1)S(1)} %copy-done.2, f32[8,2,8,64,320]{4,3,2,1,0:T(8,128)} %get-tuple-element.10, f32[8,2,8,64]{3,2,1,0:T(8,128)S(1)} %get-tuple-element.9), kind=kOutput, calls=%fused_computation.31 | convolution fusion | flops 693117248 | bytes 24412160 | tf_op jit(solution)/shard_map/ckgij,cjkd->cikgd/dot_general | solution.py:77
  493.0 3.0 copy.67
  496.0 2.3 reshape.106
  498.3 241.5 %all-reduce.3.cloned.1.call-done = f32[5120,2,256]{2,1,0:T(2,128)} async-done(((f32[5120,2,256]{2,1,0:T(2,128)}), f32[5120,2,256]{2,1,0:T(2,128)}) %all-reduce.3.cloned.1.call-update) | async-done | bytes 10485776
  739.8 2.8 constant_dynamic-slice_fusion
  742.6 12.2 %reduce-scatter.8.cloned.1.call-done = bf16[8,64,2560]{2,1,0:T(8,128)(2,1)} async-done(((bf16[8,64,5120]{2,1,0:T(8,128)(2,1)}), bf16[8,64,2560]{2,1,0:T(8,128)(2,1)}) %reduce-scatter.8.cloned.1.call-update) | async-done | bytes 2621456 | tf_op jit(solution)/shard_map/reduce_scatter | solution.py:123
  754.8 17.3 %reduce-scatter.6.cloned.1.call-done = bf16[2,256,2560]{2,1,0:T(8,128)(2,1)} async-done(((bf16[2,256,5120]{2,1,0:T(8,128)(2,1)}), bf16[2,256,2560]{2,1,0:T(8,128)(2,1)}) %reduce-scatter.6.cloned.1.call-update) | async-done | bytes 2621456 | tf_op jit(solution)/shard_map/reduce_scatter | solution.py:120
  (67 shorter events, 24.7 us)
Async XLA Ops:
  7.2 92.0 %all-gather.3.cloned.1.call-start = ((), (), s32[]{:S(2)}) async-start(), calls=%async_computation.3 | async-start | bytes 5898240 | tf_op jit(solution)/shard_map/all_gather | solution.py:10
  7.2 97.8 %slice-start = ((s8[5242880]{0:T(1024)(128)(4,1)}), s8[1048576]{0:T(1024)(128)(4,1)S(1)}, s32[]{:S(2)}) async-start(s8[5242880]{0:T(1024)(128)(4,1)} %bitcast.131), calls=%async_computation.9 | async-start | bytes 2097152
  7.9 172.8 %all-gather.5.cloned.1.call-start = ((), (), s32[]{:S(2)}) async-start(), calls=%async_computation.4 | async-start | bytes 4718592 | tf_op jit(solution)/shard_map/all_gather | solution.py:29
  99.2 5.8 slice-start.1
  102.7 2.3 copy-start
  108.0 6.7 copy-start.6
  108.0 6.7 copy-start.7
  108.9 274.9 %reduce-scatter.4.cloned.1.call-start = ((), (), s32[]{:S(2)}) async-start(), calls=%async_computation.5 | async-start | bytes 4718592 | tf_op jit(solution)/shard_map/reduce_scatter | solution.py:92
  125.2 68.4 %copy-start.3 = (bf16[8,64,2,128]{3,1,2,0:T(8,128)(2,1)}, bf16[8,64,2,128]{3,1,2,0:T(8,128)(2,1)S(1)}, u32[]{:S(2)}) copy-start(bf16[8,64,2,128]{3,1,2,0:T(8,128)(2,1)S(1)} %copy_bitcast_fusion) | copy-start | bytes 786436
  297.5 442.3 %all-reduce.3.cloned.1.call-start = ((), (), s32[]{:S(2)}) async-start(), calls=%async_computation.8 | async-start | bytes 20971520
  297.7 92.8 %slice-start.2 = ((s8[5242880]{0:T(1024)(128)(4,1)}), s8[1048576]{0:T(1024)(128)(4,1)S(1)}, s32[]{:S(2)}) async-start(s8[5242880]{0:T(1024)(128)(4,1)} %bitcast.139), calls=%async_computation.11 | async-start | bytes 2097152
  385.5 5.1 slice-start.3
  412.5 342.3 %reduce-scatter.8.cloned.1.call-start = ((), (), s32[]{:S(2)}) async-start(), calls=%async_computation.7 | async-start | bytes 7864320 | tf_op jit(solution)/shard_map/reduce_scatter | solution.py:123
  419.7 352.4 %reduce-scatter.6.cloned.1.call-start = ((), (), s32[]{:S(2)}) async-start(), calls=%async_computation.6 | async-start | bytes 7864320 | tf_op jit(solution)/shard_map/reduce_scatter | solution.py:120
  426.8 0.7 copy-start.8
  426.8 1.9 copy-start.1
  426.8 1.9 copy-start.5
  434.6 3.7 copy-start.2
  434.6 3.7 copy-start.4
Sparse Core Ops, SparseCore 0:
  10.2 88.9 all-gather.2
  109.0 71.5 all-gather.4
  297.6 86.1 reduce-scatter.3
  412.6 327.1 all-reduce.2
  742.5 12.2 reduce-scatter.7
  757.6 14.4 reduce-scatter.5
where the time goes:
time: 787 us; the launch traced here: 779 us
  waiting for transfers between devices  504 us (64%)
  matrix products  174 us (22%)
  local copies, waits for them, and re-layouts  77.6 us (10%)
  between operations  15.3 us (2%)
  other arithmetic  8.07 us (1%)
    unnamed x7, waiting for transfers between devices  242 us
    all_gather x1, waiting for transfers between devices, shards(): weights_all = lax.all_gather(kv_weight, 'dp', axis=0, tiled=True)  91.2 us
    reduce_scatter x1, waiting for transfers between devices, shards(): lax.psum_scatter(jnp.einsum('pc,clkw->plkw', row_hit, prompt_terms, prefe...  85.5 us
    dot_general x1, matrix products, shards(): jnp.einsum('ckgij,cikgd->cjkd', score_grad, query_blocks, preferred_eleme...  57.9 us
    all_gather x1, waiting for transfers between devices, shards(): everything = lax.all_gather(prompt_kv, 'dp', axis=0, tiled=True)  55.4 us
    dot_general x1, matrix products, shards(): jnp.einsum('ckgij,cjkd->cikgd', score_grad, key_rows, preferred_element_t...  54.7 us
    reduce_scatter x1, waiting for transfers between devices, shards(): lax.psum_scatter(prompt_part.astype(jnp.bfloat16), 'mp', scatter_dimensio...  17.3 us
    reshape x1, local copies, waits for them, and re-layouts, shards(): (prompt_term + own_term).reshape(model_dim // holders * lax.axis_size('dp...  16.1 us
  transfers between devices with their start and end apart: 6, of which 6 were waited for; matrix products, arithmetic and copies ran while one was open for 13% of the time, Pallas kernels for 0%

commit v1 on v0

v1 whole, which is shorter than its diff:
```python
import functools

import jax
import jax.numpy as jnp
from jax import lax
from jax.experimental import pallas as pl
from jax.experimental.pallas import tpu as pltpu
from jax.sharding import PartitionSpec as P

HEAD_DIM = 128
MESH = pl.DeviceIdType.MESH
F32 = jnp.float32
BF16 = jnp.bfloat16
VMEM_LIMIT = 60 * 1024 * 1024
NT = (((1,), (1,)), ((), ()))
TN = (((0,), (0,)), ((), ()))


def place_of(index, n):
    side = index % 2
    row = index // 2
    return row + side * (n - 1 - 2 * row)


def index_at(place, n):
    place = (place + 2 * n) % n
    back = place // (n // 2)
    return 2 * (place + back * (n - 1 - 2 * place)) + back


def enter(peers):
    barrier = pltpu.get_barrier_semaphore()
    for peer in peers:
        pl.semaphore_signal(barrier, inc=1, device_id=peer, device_id_type=MESH)
    pl.semaphore_wait(barrier, len(peers))


class Ring:
    def __init__(self, buf, send, recv, n):
        self.buf, self.send, self.recv, self.n = buf, send, recv, n
        self.half = buf.shape[1] // 2
        self.place = place_of(lax.axis_index("dp"), n)
        self.copies = []

    def owner(self, way, step):
        return index_at(self.place - step if way == 0 else self.place + step, self.n)

    def pieces(self, way, step):
        if step < self.n // 2 - 1:
            return (0, 1) if way == 0 else (1, 0)
        return (way,)

    def copy(self, way, step, piece):
        to = index_at(self.place + 1 if way == 0 else self.place - 1, self.n)
        block = self.buf.at[self.owner(way, step), pl.ds(piece * self.half, self.half)]
        return pltpu.make_async_remote_copy(
            src_ref=block,
            dst_ref=block,
            send_sem=self.send.at[way, step, piece],
            recv_sem=self.recv.at[way, step, piece],
            device_id={"dp": to},
            device_id_type=MESH,
        )

    def landed(self, way, step, piece):
        block = self.buf.at[self.owner(way, step + 1), pl.ds(piece * self.half, self.half)]
        pltpu.make_async_remote_copy(
            src_ref=block,
            dst_ref=block,
            send_sem=self.send.at[way, step, piece],
            recv_sem=self.recv.at[way, step, piece],
            device_id={"dp": self.owner(1, 1)},
            device_id_type=MESH,
        ).wait_recv()

    def run(self, use):
        last = self.n // 2
        for step in range(last + 1):
            for order in range(2):
                for way in range(2):
                    if step > 0:
                        came = self.pieces(way, step - 1)
                        if order < len(came):
                            self.landed(way, step - 1, came[order])
                    if step < last:
                        going = self.pieces(way, step)
                        if order < len(going):
                            copy = self.copy(way, step, going[order])
                            copy.start()
                            self.copies.append(copy)
            if step == 0 or step == last:
                use([self.owner(0, step)], step)
            else:
                use([self.owner(0, step), self.owner(1, step)], step)

    def finish(self):
        for copy in self.copies:
            copy.wait_send()


def project_kernel(n, w_ref, ph_ref, oh_ref, wall_ref, pkv_ref, own_ref, acc, send_w, recv_w, send_k, recv_k):
    me = lax.axis_index("dp")
    place = place_of(me, n)
    depth = w_ref.shape[0]
    rows = ph_ref.shape[0]
    tile = min(256, rows)
    wall_ref[me] = w_ref[...]
    enter([{"dp": index_at(place + 1, n)}, {"dp": index_at(place - 1, n)}])
    ring = Ring(wall_ref, send_w, recv_w, n)

    def add(owners, step):
        for source, base in ((ph_ref, 0), (oh_ref, rows)):

            @pl.loop(0, rows // tile)
            def _(r):
                at = pl.multiple_of(r * tile, tile)
                total = None
                for owner in owners:
                    cols = pl.ds(pl.multiple_of(owner * depth, 128), depth)
                    term = jnp.dot(source[pl.ds(at, tile), cols], wall_ref[owner], preferred_element_type=F32)
                    total = term if total is None else total + term
                to = pl.ds(base + at, tile)
                if step == 0:
                    acc[to] = total
                else:
                    acc[to] += total

    ring.run(add)
    pkv_ref[me] = acc[:rows].astype(BF16)
    second = Ring(pkv_ref, send_k, recv_k, n)
    second.run(lambda owners, step: None)
    own_ref[...] = acc[rows:].astype(BF16)
    ring.finish()
    second.finish()


def project(w, ph, oh, n):
    depth, width = w.shape
    rows = ph.shape[0]
    sems = pltpu.SemaphoreType.DMA((2, n // 2, 2))
    vmem = pl.BlockSpec(memory_space=pltpu.VMEM)
    return pl.pallas_call(
        functools.partial(project_kernel, n),
        out_shape=(
            jax.ShapeDtypeStruct((n, depth, width), BF16),
            jax.ShapeDtypeStruct((n, rows, width), BF16),
            jax.ShapeDtypeStruct((oh.shape[0], width), BF16),
        ),
        in_specs=[vmem] * 3,
        out_specs=(vmem,) * 3,
        scratch_shapes=[pltpu.VMEM((rows + oh.shape[0], width), F32), sems, sems, sems, sems],
        compiler_params=pltpu.CompilerParams(collective_id=0, has_side_effects=True, vmem_limit_bytes=VMEM_LIMIT),
        name="project_gather",
    )(w, ph, oh)


def attend_kernel(prompt_of, lens, pkv, own, q, cot, att, gq, terms, own_g):
    c = pl.program_id(0)
    length = lens[c]
    slots = own.shape[1]
    width = own.shape[2] // 2
    kv_heads = width // HEAD_DIM
    group = q.shape[2] // HEAD_DIM // kv_heads
    scale = HEAD_DIM ** (-0.5)
    live = lax.broadcasted_iota(jnp.int32, (slots, HEAD_DIM), 0) < length
    cols = group * slots
    key_id = lax.broadcasted_iota(jnp.int32, (slots, cols), 0)
    row_id = lax.broadcasted_iota(jnp.int32, (slots, cols), 1) % slots
    allowed = key_id <= row_id
    for k in range(kv_heads):
        ks = slice(k * HEAD_DIM, (k + 1) * HEAD_DIM)
        vs = slice(width + k * HEAD_DIM, width + (k + 1) * HEAD_DIM)
        kp, ko, vp, vo = pkv[0, :, ks], own[0, :, ks], pkv[0, :, vs], own[0, :, vs]
        heads = [slice((k * group + g) * HEAD_DIM, (k * group + g + 1) * HEAD_DIM) for g in range(group)]
        qk = jnp.concatenate([q[0, :, h] for h in heads], axis=0)
        do = jnp.concatenate(
            [jnp.where(live, cot[0, :, h].astype(F32), 0.0).astype(BF16) for h in heads], axis=0
        )
        sp = lax.dot_general(kp, qk, NT, preferred_element_type=F32)
        so = lax.dot_general(ko, qk, NT, preferred_element_type=F32)
        so = jnp.where(allowed, so, -1e30)
        top = jnp.maximum(jnp.max(sp, axis=0, keepdims=True), jnp.max(so, axis=0, keepdims=True))
        ep = jnp.exp((sp - top) * scale)
        eo = jnp.exp((so - top) * scale)
        inv = 1.0 / (jnp.sum(ep, axis=0, keepdims=True) + jnp.sum(eo, axis=0, keepdims=True))
        pp = ep * inv
        po = eo * inv
        wp = pp.astype(BF16)
        wo = po.astype(BF16)
        dp = lax.dot_general(vp, do, NT, preferred_element_type=F32)
        dn = lax.dot_general(vo, do, NT, preferred_element_type=F32)
        delta = jnp.sum(pp * dp, axis=0, keepdims=True) + jnp.sum(po * dn, axis=0, keepdims=True)
        gp = (pp * (dp - delta) * scale).astype(BF16)
        go = (po * (dn - delta) * scale).astype(BF16)
        mixed = lax.dot_general(vp, wp, TN, preferred_element_type=F32) + lax.dot_general(
            vo, wo, TN, preferred_element_type=F32
        )
        dq = lax.dot_general(kp, gp, TN, preferred_element_type=F32) + lax.dot_general(
            ko, go, TN, preferred_element_type=F32
        )
        mixed = mixed.T
        dq = dq.T
        for g, h in enumerate(heads):
            rows = slice(g * slots, (g + 1) * slots)
            att[0, :, h] = jnp.where(live, mixed[rows], 0.0).astype(BF16)
            gq[0, :, h] = dq[rows].astype(BF16)
        terms[0, :, ks] = jnp.dot(gp, qk, preferred_element_type=F32).astype(BF16)
        terms[0, :, vs] = jnp.dot(wp, do, preferred_element_type=F32).astype(BF16)
        own_g[0, :, ks] = jnp.dot(go, qk, preferred_element_type=F32).astype(BF16)
        own_g[0, :, vs] = jnp.dot(wo, do, preferred_element_type=F32).astype(BF16)


def attend(prompt_of, lens, pkv, own, q, cot, n):
    comps, slots, features = q.shape
    prompts, plen, width = pkv.shape
    per = prompts // n
    one = lambda c, p, l: (c, 0, 0)
    wide = pl.BlockSpec((1, slots, features), one)
    thin = pl.BlockSpec((1, slots, width), one)
    return pl.pallas_call(
        attend_kernel,
        out_shape=(
            jax.ShapeDtypeStruct(q.shape, BF16),
            jax.ShapeDtypeStruct(q.shape, BF16),
            jax.ShapeDtypeStruct((n, plen, width), BF16),
            jax.ShapeDtypeStruct((comps, slots, width), BF16),
        ),
        grid_spec=pltpu.PrefetchScalarGridSpec(
            num_scalar_prefetch=2,
            grid=(comps,),
            in_specs=[pl.BlockSpec((1, plen, width), lambda c, p, l: (p[c], 0, 0)), thin, wide, wide],
            out_specs=(wide, wide, pl.BlockSpec((1, plen, width), lambda c, p, l: (p[c] // per, 0, 0)), thin),
        ),
        compiler_params=pltpu.CompilerParams(vmem_limit_bytes=VMEM_LIMIT),
        name="attend",
    )(prompt_of, lens, pkv, own, q, cot)


def swap_kernel(n, src, dst, send, recv, here):
    me = lax.axis_index("dp")
    place = place_of(me, n)
    peers = [index_at(place + d, n) for d in range(1, n)]
    own = pltpu.make_async_copy(src.at[me], dst.at[me], here)
    own.start()
    enter([{"dp": peer} for peer in peers])
    order = sorted(range(1, n), key=lambda d: -min(d, n - d))
    copies = []
    for d in order:
        peer = peers[d - 1]
        copy = pltpu.make_async_remote_copy(
            src_ref=src.at[peer],
            dst_ref=dst.at[me],
            send_sem=send.at[d],
            recv_sem=recv.at[d],
            device_id={"dp": peer},
            device_id_type=MESH,
        )
        copy.start()
        copies.append(copy)
    own.wait()
    for d in order:
        came = index_at(place - d, n)
        pltpu.make_async_remote_copy(
            src_ref=dst.at[came],
            dst_ref=dst.at[came],
            send_sem=send.at[d],
            recv_sem=recv.at[d],
            device_id={"dp": peers[0]},
            device_id_type=MESH,
        ).wait_recv()
    for copy in copies:
        copy.wait_send()


def swap(terms, n):
    vmem = pl.BlockSpec(memory_space=pltpu.VMEM)
    return pl.pallas_call(
        functools.partial(swap_kernel, n),
        out_shape=jax.ShapeDtypeStruct(terms.shape, terms.dtype),
        in_specs=[vmem],
        out_specs=vmem,
        scratch_shapes=[
            pltpu.SemaphoreType.DMA((n,)),
            pltpu.SemaphoreType.DMA((n,)),
            pltpu.SemaphoreType.DMA,
        ],
        compiler_params=pltpu.CompilerParams(collective_id=1, has_side_effects=True, vmem_limit_bytes=VMEM_LIMIT),
        name="swap_terms",
    )(terms)


def grads_kernel(
    n, chunk, g_ref, gt_ref, ph_ref, oh_ref, wall_ref, fp_ref, fo_ref, gw_ref,
    slots, fsend, frecv, send, recv, send_f, recv_f,
):
    me = lax.axis_index("dp")
    mp = lax.axis_index("mp")
    place = place_of(me, n)
    right = index_at(place + 1, n)
    left = index_at(place - 1, n)
    other = {"mp": 1 - mp}
    rows = ph_ref.shape[0]
    depth = gw_ref.shape[0]
    half = gt_ref.shape[0] // 2
    last = n // 2
    chunks = fsend.shape[0]
    tile = min(256, rows)
    enter([{"dp": right}, {"dp": left}, other])

    def partial(target, piece):
        cols = pl.ds(pl.multiple_of(target * depth, 128), depth)
        top = gt_ref[piece * half : (piece + 1) * half]
        return jnp.dot(top[:, :rows], ph_ref[:, cols], preferred_element_type=F32) + jnp.dot(
            top[:, rows:], oh_ref[:, cols], preferred_element_type=F32
        )

    def copy(way, step, piece):
        return pltpu.make_async_remote_copy(
            src_ref=slots.at[way, step, piece],
            dst_ref=slots.at[way, step + 1, piece],
            send_sem=send.at[way, step, piece],
            recv_sem=recv.at[way, step, piece],
            device_id={"dp": right if way == 0 else left},
            device_id_type=MESH,
        )

    started = []

    def go(way, step, piece):
        one = copy(way, step, piece)
        one.start()
        started.append(one)

    far = index_at(place + last, n)
    for way in range(2):
        slots[way, 0, way] = partial(far, way)
        go(way, 0, way)
    for way in range(2):
        near = index_at(place + (last - 1) if way == 0 else place - (last - 1), n)
        slots[way, 1, 1 - way] = partial(near, 1 - way)
        go(way, 1, 1 - way)

    def product(first, at):
        return lax.dot_general(
            g_ref[pl.ds(at, tile)], wall_ref[pl.ds(first, chunk)], NT, preferred_element_type=F32
        ).astype(BF16)

    feature = []
    span = chunk * chunks
    for j in range(chunks):
        first = pl.multiple_of((1 - mp) * span + j * chunk, 128)

        @pl.loop(0, 2 * rows // tile)
        def _(r):
            at = pl.multiple_of(r * tile, tile)
            fsend[j, pl.ds(at, tile)] = product(first, at)

        one = pltpu.make_async_remote_copy(
            src_ref=fsend.at[j],
            dst_ref=frecv.at[j],
            send_sem=send_f.at[j],
            recv_sem=recv_f.at[j],
            device_id=other,
            device_id_type=MESH,
        )
        one.start()
        feature.append(one)
    for j in range(chunks):
        first = pl.multiple_of(mp * span + j * chunk, 128)
        feature[j].wait_recv()

        @pl.loop(0, rows // tile)
        def _(r):
            at = pl.multiple_of(r * tile, tile)
            cols = slice(j * chunk, (j + 1) * chunk)
            got = frecv[j, pl.ds(at, tile)].astype(F32)
            fp_ref[pl.ds(at, tile), cols] = (product(first, at).astype(F32) + got).astype(BF16)
            low = pl.multiple_of(rows + at, tile)
            got = frecv[j, pl.ds(low, tile)].astype(F32)
            fo_ref[pl.ds(at, tile), cols] = (product(first, low).astype(F32) + got).astype(BF16)

    for step in range(1, last):
        for order in range(2):
            for way in range(2):
                piece = way if order == 0 else 1 - way
                if step == 1 and piece != way:
                    continue
                target = index_at(place + (last - step) if way == 0 else place - (last - step), n)
                copy(way, step - 1, piece).wait_recv()
                slots[way, step, piece] += partial(target, piece)
                go(way, step, piece)
    for piece in range(2):
        mine = partial(me, piece)
        for way in range(2):
            copy(way, last - 1, piece).wait_recv()
        total = mine + slots[0, last, piece] + slots[1, last, piece]
        gw_ref[:, piece * half : (piece + 1) * half] = total.T
    for one in started:
        one.wait_send()
    for one in feature:
        one.wait_send()


def grads(g, ph, oh, wall, n, n_mp):
    rows, model_dim = ph.shape
    width = g.shape[1]
    depth = model_dim // n
    share = model_dim // n_mp
    chunk = 512 if share % 512 == 0 else 128
    chunks = share // chunk
    vmem = pl.BlockSpec(memory_space=pltpu.VMEM)
    sems = pltpu.SemaphoreType.DMA((2, n // 2, 2))
    return pl.pallas_call(
        functools.partial(grads_kernel, n, chunk),
        out_shape=(
            jax.ShapeDtypeStruct((rows, share), BF16),
            jax.ShapeDtypeStruct((rows, share), BF16),
            jax.ShapeDtypeStruct((depth, width), F32),
        ),
        in_specs=[vmem] * 5,
        out_specs=(vmem,) * 3,
        scratch_shapes=[
            pltpu.VMEM((2, n // 2 + 1, 2, width // 2, depth), F32),
            pltpu.VMEM((chunks, 2 * rows, chunk), BF16),
            pltpu.VMEM((chunks, 2 * rows, chunk), BF16),
            sems,
            sems,
            pltpu.SemaphoreType.DMA((chunks,)),
            pltpu.SemaphoreType.DMA((chunks,)),
        ],
        compiler_params=pltpu.CompilerParams(collective_id=2, has_side_effects=True, vmem_limit_bytes=VMEM_LIMIT),
        name="grads_reduce",
    )(g, g.T, ph, oh, wall)


def shards(n, n_mp, prompt_hidden, completion_hidden, queries, cotangent, kv_weight, prompt_of, comp_len):
    per, plen, model_dim = prompt_hidden.shape
    comps, slots, _ = completion_hidden.shape
    depth, _, kv_width = kv_weight.shape
    width = 2 * kv_width
    w = kv_weight.reshape(depth, width)
    ph = prompt_hidden.reshape(per * plen, model_dim)
    oh = completion_hidden.reshape(comps * slots, model_dim)
    wall, pkv, own = project(w, ph, oh, n)
    pkv = pkv.reshape(n * per, plen, width)
    attended, grad_queries, terms, own_grads = attend(
        prompt_of, comp_len.reshape(-1), pkv, own.reshape(comps, slots, width), queries, cotangent, n
    )
    got = swap(terms, n)
    everyone = lax.all_gather(prompt_of, "dp", axis=0, tiled=False)
    mine = lax.axis_index("dp") * per + jnp.arange(per, dtype=jnp.int32)
    hit = jnp.any(everyone[:, :, None] == mine[None, None, :], axis=1)
    prompt_grads = jnp.stack(
        [jnp.sum(jnp.where(hit[:, s, None, None], got.astype(F32), 0.0), axis=0) for s in range(per)]
    ).astype(BF16)
    g = jnp.concatenate([prompt_grads.reshape(per * plen, width), own_grads.reshape(comps * slots, width)], axis=0)
    fp, fo, gw = grads(g, ph, oh, wall.reshape(model_dim, width), n, n_mp)
    return (
        attended,
        grad_queries,
        fp.reshape(per, plen, -1),
        fo.reshape(comps, slots, -1),
        gw.reshape(depth, 2, kv_width),
    )


def solution(mesh):
    in_specs = (
        P(("groups", "dp"), None, None),
        P(("groups", "dp"), None, None),
        P(("groups", "dp"), None, "mp"),
        P(("groups", "dp"), None, "mp"),
        P("dp", None, "mp"),
        P(("groups", "dp")),
        P(("groups", "dp"), None),
    )
    out_specs = (P(("groups", "dp"), None, "mp"),) * 5
    body = functools.partial(shards, mesh.shape["dp"], mesh.shape["mp"])
    return jax.shard_map(body, mesh=mesh, in_specs=in_specs, out_specs=out_specs, check_vma=False)
```

time: 787 us -> 309 us (0.39)
  waiting for transfers between devices: 504 us -> 0 us
  Pallas kernels: 0 us -> 276 us
  matrix products: 174 us -> 0 us
  local copies, waits for them, and re-layouts: 77.6 us -> 14.3 us
  between operations: 15.3 us -> 1.37 us
  blocking collectives: 0 us -> 13.1 us
    pallas_call x0 -> x4, Pallas kernels: none -> 276 us  [the longest x1 116 us: grads(): pl.pallas_call(functools.partial(grads_kernel, n, chunk), out_shape=(jax....]
    unnamed x7 -> x0, waiting for transfers between devices: 242 us -> none
    dot_general x13 -> x0, matrix products: 174 us -> none  [the longest x1 57.9 us: shards(): jnp.einsum('ckgij,cikgd->cjkd', score_grad, query_blocks, preferred_eleme...]
    all_gather x2 -> x0, waiting for transfers between devices: 147 us -> none  [the longest x1 91.2 us: shards(): weights_all = lax.all_gather(kv_weight, 'dp', axis=0, tiled=True)]
    reduce_scatter x3 -> x0, waiting for transfers between devices: 115 us -> none  [the longest x1 85.5 us: shards(): lax.psum_scatter(jnp.einsum('pc,clkw->plkw', row_hit, prompt_terms, prefe...]
    reshape x6 -> x2, local copies, waits for them, and re-layouts: 21.8 us -> 4.34 us  [the longest x1 3.09 us: shards(): gw.reshape(depth, 2, kv_width)]
    another operation x4 -> x0, local copies, waits for them, and re-layouts: 13.3 us -> none  [shards(): kv_grads = jnp.stack([key_grads, value_grads], axis=2)]
    unnamed x0 -> x1, blocking collectives: none -> 13.1 us
  transfers between devices with their start and end apart: 6 -> 0, of which waited for: 6 -> 0; matrix products, arithmetic and copies ran while one was open for 13% -> 0% of each run, Pallas kernels for 0% -> 0%
where the time goes in v1:
time: 309 us; the launch traced here: 308 us
  Pallas kernels  276 us (89%)
  local copies, waits for them, and re-layouts  14.3 us (5%)
  blocking collectives  13.1 us (4%)
  other arithmetic  3.88 us (1%)
    pallas_call x1, Pallas kernels, grads(): pl.pallas_call(functools.partial(grads_kernel, n, chunk), out_shape=(jax....  116 us
    pallas_call x1, Pallas kernels, project(): pl.pallas_call(functools.partial(project_kernel, n), out_shape=(jax.Shape...  97 us
    pallas_call x1, Pallas kernels, swap(): pl.pallas_call(functools.partial(swap_kernel, n), out_shape=jax.ShapeDtyp...  43.9 us
    pallas_call x1, Pallas kernels, attend(): pl.pallas_call(attend_kernel, out_shape=(jax.ShapeDtypeStruct(q.shape, BF...  18.4 us
    unnamed x1, blocking collectives  13.1 us
    unnamed x10, local copies, waits for them, and re-layouts  8.32 us

profile of v1, /device:TPU:0, one launch (start us, length us, event | category | flops | bytes accessed | tf_op | source)
XLA Modules:
  0.0 308.3 jit_solution(11288003826795018111)
XLA Ops:
  0.6 1.2 dynamic-slice
  2.6 0.9 dynamic-update-slice
  3.4 13.1 %all-reduce = s32[64]{0:T(128)S(1)} all-reduce(s32[64]{0:T(128)S(1)} %dynamic-update-slice), channel_id=2, replica_groups=mesh['groups'=2,'dp'=8,'mp'=2] {'dp'}, use_global_device_ids=true, to_apply=%add | all-reduce | flops 64 | bytes 512
  16.5 0.1 reshape.64
  16.5 0.2 compare_reduce_fusion
  16.8 2.0 copy.21
  18.8 97.0 %project_gather.1 = (bf16[8,640,512]{2,1,0:T(8,128)(2,1)}, bf16[8,512,512]{2,1,0:T(8,128)(2,1)}, bf16[512,512]{1,0:T(8,128)(2,1)}) custom-call(bf16[640,512]{1,0:T(8,128)(2,1)} %bitcast.33, bf16[512,5120]{1,0:T(8,128)(2,1)} %bitcast.25, bf16[512,5120]{1,0:T(8,128)(2,1)} %bitcast.27), custom_call_target="tpu_custom_call" | custom-call | tf_op jit(solution)/shard_map/project_gather/pallas_call | solution.py:142
  115.8 18.4 %attend.1 = (bf16[8,64,2048]{2,1,0:T(8,128)(2,1)}, bf16[8,64,2048]{2,1,0:T(8,128)(2,1)}, bf16[8,256,512]{2,1,0:T(8,128)(2,1)}, bf16[8,64,512]{2,1,0:T(8,128)(2,1)}) custom-call(s32[8]{0:T(128)} %prompt_of.1, s32[8]{0:T(128)} %bitcast.40, bf16[16,256,512]{2,1,0:T(8,128)(2,1)} %bitcast.30, bf16[8,64,512]{2,1,0:T(8,128)(2,1)} %bitcast.38, ...), custom_call_target="tpu_custom_call" | custom-call | tf_op jit(solution)/shard_map/attend/pallas_call | solution.py:220
  134.2 1.3 copy.18
  135.4 43.9 %swap_terms.1 = bf16[8,256,512]{2,1,0:T(8,128)(2,1)} custom-call(bf16[8,256,512]{2,1,0:T(8,128)(2,1)} %get-tuple-element.19.src), custom_call_target="tpu_custom_call" | custom-call | tf_op jit(solution)/shard_map/swap_terms/pallas_call | solution.py:277
  179.3 2.4 fusion
  181.7 0.1 pad_maximum_fusion.1
  181.8 0.2 copy.20
  182.0 1.2 fusion.2
  183.2 1.3 copy.19.g_ref
  184.6 116.5 %grads_reduce.1 = (bf16[512,2560]{1,0:T(8,128)(2,1)}, bf16[512,2560]{1,0:T(8,128)(2,1)}, f32[640,512]{1,0:T(8,128)}) custom-call(bf16[1024,512]{1,0:T(8,128)(2,1)} %copy.19.g_ref, bf16[512,1024]{1,0:T(8,128)(2,1)} %get-tuple-element.27.gt_ref, bf16[512,5120]{1,0:T(8,128)(2,1)} %bitcast.26, bf16[512,5120]{1,0:T(8,128)(2,1)} %bitcast.28, ...), custom_call_target="tpu_custom_call" | custom-call | tf_op jit(solution)/shard_map/grads_reduce/pallas_call | solution.py:413
  301.1 0.0 copy-start.1
  301.1 3.1 %reshape.63 = f32[640,2,256]{2,1,0:T(2,128)} reshape(f32[640,512]{1,0:T(8,128)} %get-tuple-element.24) | data formatting | bytes 2621440 | tf_op jit(solution)/shard_map/reshape | solution.py:463
  304.2 0.0 copy-done.1
  304.2 0.0 copy-start
  304.2 1.5 copy.25
  305.7 1.2 copy-done
  306.8 1.5 copy.26
  (3 shorter events, 0.0 us)
Async XLA Ops:
  301.1 3.1 %copy-start.1 = (bf16[512,2560]{1,0:T(8,128)(2,1)S(1)}, bf16[512,2560]{1,0:T(8,128)(2,1)}, u32[]{:S(2)}) copy-start(bf16[512,2560]{1,0:T(8,128)(2,1)} %get-tuple-element.22) | copy-start | bytes 7864324
  304.2 2.7 copy-start

commit v2 on v1

--- a/solution.py
+++ b/solution.py
@@ -14,6 +14,8 @@
 VMEM_LIMIT = 60 * 1024 * 1024
 NT = (((1,), (1,)), ((), ()))
 TN = (((0,), (0,)), ((), ()))
+EXTRA = 16
+STEPS = 32000.0
 
 
 def place_of(index, n):
@@ -98,17 +100,28 @@
             copy.wait_send()
 
 
-def project_kernel(n, w_ref, ph_ref, oh_ref, wall_ref, pkv_ref, own_ref, acc, send_w, recv_w, send_k, recv_k):
+def project_kernel(
+    n, w_ref, ph_hbm, oh_hbm, wall_ref, pkv_ref, own_ref, ph_ref, oh_ref, acc, load, send_w, recv_w, send_k, recv_k
+):
     me = lax.axis_index("dp")
     place = place_of(me, n)
     depth = w_ref.shape[0]
     rows = ph_ref.shape[0]
     tile = min(256, rows)
+    loads = [
+        pltpu.make_async_copy(src, dst, load.at[i])
+        for i, (src, dst) in enumerate(((ph_hbm, ph_ref), (oh_hbm, oh_ref)))
+    ]
+    for one in loads:
+        one.start()
     wall_ref[me] = w_ref[...]
     enter([{"dp": index_at(place + 1, n)}, {"dp": index_at(place - 1, n)}])
     ring = Ring(wall_ref, send_w, recv_w, n)
 
     def add(owners, step):
+        if step == 0:
+            for one in loads:
+                one.wait()
         for source, base in ((ph_ref, 0), (oh_ref, rows)):
 
             @pl.loop(0, rows // tile)
@@ -146,16 +159,27 @@
             jax.ShapeDtypeStruct((n, rows, width), BF16),
             jax.ShapeDtypeStruct((oh.shape[0], width), BF16),
         ),
-        in_specs=[vmem] * 3,
+        in_specs=[vmem] + [pl.BlockSpec(memory_space=pl.ANY)] * 2,
         out_specs=(vmem,) * 3,
-        scratch_shapes=[pltpu.VMEM((rows + oh.shape[0], width), F32), sems, sems, sems, sems],
+        scratch_shapes=[
+            pltpu.VMEM(ph.shape, BF16),
+            pltpu.VMEM(oh.shape, BF16),
+            pltpu.VMEM((rows + oh.shape[0], width), F32),
+            pltpu.SemaphoreType.DMA((2,)),
+            sems,
+            sems,
+            sems,
+            sems,
+        ],
         compiler_params=pltpu.CompilerParams(collective_id=0, has_side_effects=True, vmem_limit_bytes=VMEM_LIMIT),
         name="project_gather",
     )(w, ph, oh)
 
 
-def attend_kernel(prompt_of, lens, pkv, own, q, cot, att, gq, terms, own_g):
+def attend_kernel(per, prompt_of, lens, pkv, own, q, cot, *rest):
+    att, gq, terms, own_g = rest[-4:]
     c = pl.program_id(0)
+    plen = pkv.shape[1]
     length = lens[c]
     slots = own.shape[1]
     width = own.shape[2] // 2
@@ -167,6 +191,8 @@
     key_id = lax.broadcasted_iota(jnp.int32, (slots, cols), 0)
     row_id = lax.broadcasted_iota(jnp.int32, (slots, cols), 1) % slots
     allowed = key_id <= row_id
+    mark = (prompt_of[c] % per + 1).astype(F32)
+    terms[0, plen:] = jnp.full((EXTRA, 2 * width), mark, F32).astype(BF16)
     for k in range(kv_heads):
         ks = slice(k * HEAD_DIM, (k + 1) * HEAD_DIM)
         vs = slice(width + k * HEAD_DIM, width + (k + 1) * HEAD_DIM)
@@ -204,8 +230,8 @@
             rows = slice(g * slots, (g + 1) * slots)
             att[0, :, h] = jnp.where(live, mixed[rows], 0.0).astype(BF16)
             gq[0, :, h] = dq[rows].astype(BF16)
-        terms[0, :, ks] = jnp.dot(gp, qk, preferred_element_type=F32).astype(BF16)
-        terms[0, :, vs] = jnp.dot(wp, do, preferred_element_type=F32).astype(BF16)
+        terms[0, :plen, ks] = jnp.dot(gp, qk, preferred_element_type=F32).astype(BF16)
+        terms[0, :plen, vs] = jnp.dot(wp, do, preferred_element_type=F32).astype(BF16)
         own_g[0, :, ks] = jnp.dot(go, qk, preferred_element_type=F32).astype(BF16)
         own_g[0, :, vs] = jnp.dot(wo, do, preferred_element_type=F32).astype(BF16)
 
@@ -217,81 +243,47 @@
     one = lambda c, p, l: (c, 0, 0)
     wide = pl.BlockSpec((1, slots, features), one)
     thin = pl.BlockSpec((1, slots, width), one)
+    held = (n, plen + EXTRA, width)
+    blank = [] if n <= comps else [jnp.zeros(held, BF16)]
     return pl.pallas_call(
-        attend_kernel,
+        functools.partial(attend_kernel, per),
         out_shape=(
             jax.ShapeDtypeStruct(q.shape, BF16),
             jax.ShapeDtypeStruct(q.shape, BF16),
-            jax.ShapeDtypeStruct((n, plen, width), BF16),
+            jax.ShapeDtypeStruct(held, BF16),
             jax.ShapeDtypeStruct((comps, slots, width), BF16),
         ),
         grid_spec=pltpu.PrefetchScalarGridSpec(
             num_scalar_prefetch=2,
             grid=(comps,),
-            in_specs=[pl.BlockSpec((1, plen, width), lambda c, p, l: (p[c], 0, 0)), thin, wide, wide],
-            out_specs=(wide, wide, pl.BlockSpec((1, plen, width), lambda c, p, l: (p[c] // per, 0, 0)), thin),
+            in_specs=[pl.BlockSpec((1, plen, width), lambda c, p, l: (p[c], 0, 0)), thin, wide, wide]
+            + [pl.BlockSpec(memory_space=pl.ANY)] * len(blank),
+            out_specs=(wide, wide, pl.BlockSpec((1, plen + EXTRA, width), lambda c, p, l: (p[c] // per, 0, 0)), thin),
         ),
+        input_output_aliases={6: 2} if blank else {},
         compiler_params=pltpu.CompilerParams(vmem_limit_bytes=VMEM_LIMIT),
         name="attend",
-    )(prompt_of, lens, pkv, own, q, cot)
-
-
-def swap_kernel(n, src, dst, send, recv, here):
-    me = lax.axis_index("dp")
-    place = place_of(me, n)
-    peers = [index_at(place + d, n) for d in range(1, n)]
-    own = pltpu.make_async_copy(src.at[me], dst.at[me], here)
-    own.start()
-    enter([{"dp": peer} for peer in peers])
-    order = sorted(range(1, n), key=lambda d: -min(d, n - d))
-    copies = []
-    for d in order:
-        peer = peers[d - 1]
-        copy = pltpu.make_async_remote_copy(
-            src_ref=src.at[peer],
-            dst_ref=dst.at[me],
-            send_sem=send.at[d],
-            recv_sem=recv.at[d],
-            device_id={"dp": peer},
-            device_id_type=MESH,
-        )
-        copy.start()
-        copies.append(copy)
-    own.wait()
-    for d in order:
-        came = index_at(place - d, n)
-        pltpu.make_async_remote_copy(
-            src_ref=dst.at[came],
-            dst_ref=dst.at[came],
-            send_sem=send.at[d],
-            recv_sem=recv.at[d],
-            device_id={"dp": peers[0]},
-            device_id_type=MESH,
-        ).wait_recv()
-    for copy in copies:
-        copy.wait_send()
-
-
-def swap(terms, n):
-    vmem = pl.BlockSpec(memory_space=pltpu.VMEM)
-    return pl.pallas_call(
-        functools.partial(swap_kernel, n),
-        out_shape=jax.ShapeDtypeStruct(terms.shape, terms.dtype),
-        in_specs=[vmem],
-        out_specs=vmem,
-        scratch_shapes=[
-            pltpu.SemaphoreType.DMA((n,)),
-            pltpu.SemaphoreType.DMA((n,)),
-            pltpu.SemaphoreType.DMA,
-        ],
-        compiler_params=pltpu.CompilerParams(collective_id=1, has_side_effects=True, vmem_limit_bytes=VMEM_LIMIT),
-        name="swap_terms",
-    )(terms)
+    )(prompt_of, lens, pkv, own, q, cot, *blank)
+
+
+def encode(block, ref):
+    top = jnp.maximum(jnp.max(jnp.abs(block), axis=0, keepdims=True), 1e-30)
+    power = jnp.ceil(jnp.log2(top))
+    rows = block.shape[0]
+    ref[:rows] = jnp.round(block * (jnp.exp2(-power) * STEPS)).astype(jnp.int32).astype(jnp.int16)
+    ref[rows:] = jnp.broadcast_to(power, (EXTRA, block.shape[1])).astype(jnp.int32).astype(jnp.int16)
+
+
+def decode(ref):
+    rows = ref.shape[0] - EXTRA
+    power = ref[rows:].astype(jnp.int32).astype(F32)[:1]
+    return ref[:rows].astype(jnp.int32).astype(F32) * (jnp.exp2(power) * (1.0 / STEPS))
 
 
 def grads_kernel(
-    n, chunk, g_ref, gt_ref, ph_ref, oh_ref, wall_ref, fp_ref, fo_ref, gw_ref,
-    slots, fsend, frecv, send, recv, send_f, recv_f,
+    n, chunk, per, terms_ref, own_ref, ph_hbm, oh_hbm, wall_hbm, fp_ref, fo_ref, gw_ref,
+    got, g_ref, gt_ref, ph_ref, oh_ref, wall_ref, slots, fsend, frecv,
+    load, here, send_t, recv_t, send, recv, send_f, recv_f,
 ):
     me = lax.axis_index("dp")
     mp = lax.axis_index("mp")
@@ -300,12 +292,106 @@
     left = index_at(place - 1, n)
     other = {"mp": 1 - mp}
     rows = ph_ref.shape[0]
+    plen = rows // per
     depth = gw_ref.shape[0]
-    half = gt_ref.shape[0] // 2
+    width = gt_ref.shape[0]
+    half = width // 2
     last = n // 2
-    chunks = fsend.shape[0]
+    chunks = fsend.shape[1]
     tile = min(256, rows)
-    enter([{"dp": right}, {"dp": left}, other])
+    loads = [
+        pltpu.make_async_copy(src, dst, load.at[i])
+        for i, (src, dst) in enumerate(((wall_hbm, wall_ref), (oh_hbm, oh_ref), (ph_hbm, ph_ref)))
+    ]
+    own_copy = pltpu.make_async_copy(terms_ref.at[me], got.at[me], here)
+    own_copy.start()
+    for one in loads:
+        one.start()
+    peers = [index_at(place + d, n) for d in range(1, n)]
+    enter([{"dp": peer} for peer in peers] + [other])
+    order = sorted(range(1, n), key=lambda d: -min(d, n - d))
+    swaps = []
+    for d in order:
+        peer = peers[d - 1]
+        one = pltpu.make_async_remote_copy(
+            src_ref=terms_ref.at[peer],
+            dst_ref=got.at[me],
+            send_sem=send_t.at[d],
+            recv_sem=recv_t.at[d],
+            device_id={"dp": peer},
+            device_id_type=MESH,
+        )
+        one.start()
+        swaps.append(one)
+    span = chunk * chunks
+
+    def product(first, at):
+        return lax.dot_general(
+            g_ref[pl.ds(at, tile)], wall_ref[pl.ds(first, chunk)], NT, preferred_element_type=F32
+        ).astype(BF16)
+
+    feature = {}
+
+    def away(part):
+        for j in range(chunks):
+            first = pl.multiple_of((1 - mp) * span + j * chunk, 128)
+
+            @pl.loop(0, rows // tile)
+            def _(r):
+                at = pl.multiple_of(r * tile, tile)
+                fsend[part, j, pl.ds(at, tile)] = product(first, pl.multiple_of(part * rows + at, tile))
+
+            one = pltpu.make_async_remote_copy(
+                src_ref=fsend.at[part, j],
+                dst_ref=frecv.at[part, j],
+                send_sem=send_f.at[part, j],
+                recv_sem=recv_f.at[part, j],
+                device_id=other,
+                device_id_type=MESH,
+            )
+            one.start()
+            feature[part, j] = one
+
+    def home(part, out_ref):
+        for j in range(chunks):
+            first = pl.multiple_of(mp * span + j * chunk, 128)
+            feature[part, j].wait_recv()
+
+            @pl.loop(0, rows // tile)
+            def _(r):
+                at = pl.multiple_of(r * tile, tile)
+                mine = product(first, pl.multiple_of(part * rows + at, tile)).astype(F32)
+                total = mine + frecv[part, j, pl.ds(at, tile)].astype(F32)
+                out_ref[pl.ds(at, tile), j * chunk : (j + 1) * chunk] = total.astype(BF16)
+
+    g_ref[rows:] = own_ref[...]
+    gt_ref[:, rows:] = own_ref[...].astype(F32).T.astype(BF16)
+    loads[0].wait()
+    away(1)
+    home(1, fo_ref)
+    loads[1].wait()
+    loads[2].wait()
+    own_copy.wait()
+    for d in order:
+        came = index_at(place - d, n)
+        pltpu.make_async_remote_copy(
+            src_ref=got.at[came],
+            dst_ref=got.at[came],
+            send_sem=send_t.at[d],
+            recv_sem=recv_t.at[d],
+            device_id={"dp": peers[0]},
+            device_id_type=MESH,
+        ).wait_recv()
+    for s in range(per):
+        for lane in range(0, width, half):
+            cols = slice(lane, lane + half)
+            total = jnp.zeros((plen, half), F32)
+            for e in range(n):
+                mark = got[e, plen:, cols].astype(F32)[:1]
+                total = total + jnp.where(mark == float(s + 1), got[e, :plen, cols].astype(F32), 0.0)
+            kept = total.astype(BF16)
+            g_ref[s * plen : (s + 1) * plen, cols] = kept
+            gt_ref[cols, s * plen : (s + 1) * plen] = kept.astype(F32).T.astype(BF16)
 
     def partial(target, piece):
         cols = pl.ds(pl.multiple_of(target * depth, 128), depth)
@@ -333,104 +419,77 @@
 
     far = index_at(place + last, n)
     for way in range(2):
-        slots[way, 0, way] = partial(far, way)
+        encode(partial(far, way), slots.at[way, 0, way])
         go(way, 0, way)
     for way in range(2):
         near = index_at(place + (last - 1) if way == 0 else place - (last - 1), n)
-        slots[way, 1, 1 - way] = partial(near, 1 - way)
+        encode(partial(near, 1 - way), slots.at[way, 1, 1 - way])
         go(way, 1, 1 - way)
-
-    def product(first, at):
-        return lax.dot_general(
-            g_ref[pl.ds(at, tile)], wall_ref[pl.ds(first, chunk)], NT, preferred_element_type=F32
-        ).astype(BF16)
-
-    feature = []
-    span = chunk * chunks
-    for j in range(chunks):
-        first = pl.multiple_of((1 - mp) * span + j * chunk, 128)
-
-        @pl.loop(0, 2 * rows // tile)
-        def _(r):
-            at = pl.multiple_of(r * tile, tile)
-            fsend[j, pl.ds(at, tile)] = product(first, at)
-
-        one = pltpu.make_async_remote_copy(
-            src_ref=fsend.at[j],
-            dst_ref=frecv.at[j],
-            send_sem=send_f.at[j],
-            recv_sem=recv_f.at[j],
-            device_id=other,
-            device_id_type=MESH,
-        )
-        one.start()
-        feature.append(one)
-    for j in range(chunks):
-        first = pl.multiple_of(mp * span + j * chunk, 128)
-        feature[j].wait_recv()
-
-        @pl.loop(0, rows // tile)
-        def _(r):
-            at = pl.multiple_of(r * tile, tile)
-            cols = slice(j * chunk, (j + 1) * chunk)
-            got = frecv[j, pl.ds(at, tile)].astype(F32)
-            fp_ref[pl.ds(at, tile), cols] = (product(first, at).astype(F32) + got).astype(BF16)
-            low = pl.multiple_of(rows + at, tile)
-            got = frecv[j, pl.ds(low, tile)].astype(F32)
-            fo_ref[pl.ds(at, tile), cols] = (product(first, low).astype(F32) + got).astype(BF16)
-
+    away(0)
     for step in range(1, last):
-        for order in range(2):
+        for turn in range(2):
             for way in range(2):
-                piece = way if order == 0 else 1 - way
+                piece = way if turn == 0 else 1 - way
                 if step == 1 and piece != way:
                     continue
                 target = index_at(place + (last - step) if way == 0 else place - (last - step), n)
+                mine = partial(target, piece)
                 copy(way, step - 1, piece).wait_recv()
-                slots[way, step, piece] += partial(target, piece)
+                encode(decode(slots.at[way, step, piece]) + mine, slots.at[way, step, piece])
                 go(way, step, piece)
+        if step == 1:
+            home(0, fp_ref)
     for piece in range(2):
         mine = partial(me, piece)
         for way in range(2):
             copy(way, last - 1, piece).wait_recv()
-        total = mine + slots[0, last, piece] + slots[1, last, piece]
+        total = mine + decode(slots.at[0, last, piece]) + decode(slots.at[1, last, piece])
         gw_ref[:, piece * half : (piece + 1) * half] = total.T
-    for one in started:
+    for one in started + swaps + list(feature.values()):
         one.wait_send()
-    for one in feature:
-        one.wait_send()
-
-
-def grads(g, ph, oh, wall, n, n_mp):
+
+
+def grads(terms, own_g, ph, oh, wall, n, n_mp, per):
     rows, model_dim = ph.shape
-    width = g.shape[1]
+    width = own_g.shape[1]
     depth = model_dim // n
     share = model_dim // n_mp
     chunk = 512 if share % 512 == 0 else 128
     chunks = share // chunk
     vmem = pl.BlockSpec(memory_space=pltpu.VMEM)
+    hbm = pl.BlockSpec(memory_space=pl.ANY)
     sems = pltpu.SemaphoreType.DMA((2, n // 2, 2))
     return pl.pallas_call(
-        functools.partial(grads_kernel, n, chunk),
+        functools.partial(grads_kernel, n, chunk, per),
         out_shape=(
             jax.ShapeDtypeStruct((rows, share), BF16),
             jax.ShapeDtypeStruct((rows, share), BF16),
             jax.ShapeDtypeStruct((depth, width), F32),
         ),
-        in_specs=[vmem] * 5,
+        in_specs=[vmem, vmem, hbm, hbm, hbm],
         out_specs=(vmem,) * 3,
         scratch_shapes=[
-            pltpu.VMEM((2, n // 2 + 1, 2, width // 2, depth), F32),
-            pltpu.VMEM((chunks, 2 * rows, chunk), BF16),
-            pltpu.VMEM((chunks, 2 * rows, chunk), BF16),
+            pltpu.VMEM(terms.shape, BF16),
+            pltpu.VMEM((2 * rows, width), BF16),
+            pltpu.VMEM((width, 2 * rows), BF16),
+            pltpu.VMEM(ph.shape, BF16),
+            pltpu.VMEM(oh.shape, BF16),
+            pltpu.VMEM(wall.shape, BF16),
+            pltpu.VMEM((2, n // 2 + 1, 2, width // 2 + EXTRA, depth), jnp.int16),
+            pltpu.VMEM((2, chunks, rows, chunk), BF16),
+            pltpu.VMEM((2, chunks, rows, chunk), BF16),
+            pltpu.SemaphoreType.DMA((3,)),
+            pltpu.SemaphoreType.DMA,
+            pltpu.SemaphoreType.DMA((n,)),
+            pltpu.SemaphoreType.DMA((n,)),
             sems,
             sems,
-            pltpu.SemaphoreType.DMA((chunks,)),
-            pltpu.SemaphoreType.DMA((chunks,)),
+            pltpu.SemaphoreType.DMA((2, chunks)),
+            pltpu.SemaphoreType.DMA((2, chunks)),
         ],
         compiler_params=pltpu.CompilerParams(collective_id=2, has_side_effects=True, vmem_limit_bytes=VMEM_LIMIT),
         name="grads_reduce",
-    )(g, g.T, ph, oh, wall)
+    )(terms, own_g, ph, oh, wall)
 
 
 def shards(n, n_mp, prompt_hidden, completion_hidden, queries, cotangent, kv_weight, prompt_of, comp_len):
@@ -446,15 +505,9 @@
     attended, grad_queries, terms, own_grads = attend(
         prompt_of, comp_len.reshape(-1), pkv, own.reshape(comps, slots, width), queries, cotangent, n
     )
-    got = swap(terms, n)
-    everyone = lax.all_gather(prompt_of, "dp", axis=0, tiled=False)
-    mine = lax.axis_index("dp") * per + jnp.arange(per, dtype=jnp.int32)
-    hit = jnp.any(everyone[:, :, None] == mine[None, None, :], axis=1)
-    prompt_grads = jnp.stack(
-        [jnp.sum(jnp.where(hit[:, s, None, None], got.astype(F32), 0.0), axis=0) for s in range(per)]
-    ).astype(BF16)
-    g = jnp.concatenate([prompt_grads.reshape(per * plen, width), own_grads.reshape(comps * slots, width)], axis=0)
-    fp, fo, gw = grads(g, ph, oh, wall.reshape(model_dim, width), n, n_mp)
+    fp, fo, gw = grads(
+        terms, own_grads.reshape(comps * slots, width), ph, oh, wall.reshape(model_dim, width), n, n_mp, per
+    )
     return (
         attended,
         grad_queries,

time: 309 us -> 245 us (0.79)
  Pallas kernels: 276 us -> 235 us
  blocking collectives: 13.1 us -> 0 us
  local copies, waits for them, and re-layouts: 14.3 us -> 9.31 us
  other arithmetic: 3.88 us -> 0 us
    pallas_call x3 -> x2, Pallas kernels: 179 us -> 133 us  [the longest x1 114 us: grads(): pl.pallas_call(functools.partial(grads_kernel, n, chunk, per), out_shape=...]
    unnamed x1 -> x0, blocking collectives: 13.1 us -> none
    pallas_call x1, Pallas kernels: 97 us -> 102 us  [project(): pl.pallas_call(functools.partial(project_kernel, n), out_shape=(jax.Shape...]
    unnamed x10 -> x7, local copies, waits for them, and re-layouts: 8.32 us -> 6.21 us
where the time goes in v2:
time: 245 us
  Pallas kernels  235 us (96%)
  local copies, waits for them, and re-layouts  9.31 us (4%)
    pallas_call x1, Pallas kernels, grads(): pl.pallas_call(functools.partial(grads_kernel, n, chunk, per), out_shape=...  114 us
    pallas_call x1, Pallas kernels, project(): pl.pallas_call(functools.partial(project_kernel, n), out_shape=(jax.Shape...  102 us
    pallas_call x1, Pallas kernels, attend(): pl.pallas_call(functools.partial(attend_kernel, per), out_shape=(jax.Shap...  18.4 us
    unnamed x7, local copies, waits for them, and re-layouts  6.21 us

profile of v2, /device:TPU:0, one launch (start us, length us, event | category | flops | bytes accessed | tf_op | source)
XLA Modules:
  0.0 244.7 jit_solution(5793271644044059534)
XLA Ops:
  0.6 2.0 copy.12
  2.7 102.0 %project_gather.1 = (bf16[8,640,512]{2,1,0:T(8,128)(2,1)}, bf16[8,512,512]{2,1,0:T(8,128)(2,1)}, bf16[512,512]{1,0:T(8,128)(2,1)}) custom-call(bf16[640,512]{1,0:T(8,128)(2,1)} %bitcast.19, bf16[512,5120]{1,0:T(8,128)(2,1)} %bitcast.11, bf16[512,5120]{1,0:T(8,128)(2,1)} %bitcast.13), custom_call_target="tpu_custom_call" | custom-call | tf_op jit(solution)/shard_map/project_gather/pallas_call | solution.py:155
  104.7 18.4 %attend.1 = (bf16[8,64,2048]{2,1,0:T(8,128)(2,1)}, bf16[8,64,2048]{2,1,0:T(8,128)(2,1)}, bf16[8,272,512]{2,1,0:T(8,128)(2,1)}, bf16[8,64,512]{2,1,0:T(8,128)(2,1)}) custom-call(s32[8]{0:T(128)} %prompt_of.1, s32[8]{0:T(128)} %bitcast.23, bf16[16,256,512]{2,1,0:T(8,128)(2,1)} %bitcast.16, bf16[8,64,512]{2,1,0:T(8,128)(2,1)} %bitcast.22, ...), custom_call_target="tpu_custom_call" | custom-call | tf_op jit(solution)/shard_map/attend/pallas_call | solution.py:248
  123.1 114.4 %grads_reduce.1 = (bf16[512,2560]{1,0:T(8,128)(2,1)}, bf16[512,2560]{1,0:T(8,128)(2,1)}, f32[640,512]{1,0:T(8,128)}) custom-call(bf16[8,272,512]{2,1,0:T(8,128)(2,1)} %get-tuple-element.19.terms_ref, bf16[512,512]{1,0:T(8,128)(2,1)} %bitcast.21, bf16[512,5120]{1,0:T(8,128)(2,1)} %bitcast.12, bf16[512,5120]{1,0:T(8,128)(2,1)} %bitcast.14, ...), custom_call_target="tpu_custom_call" | custom-call | tf_op jit(solution)/shard_map/grads_reduce/pallas_call | solution.py:462
  237.4 0.0 copy-start.1
  237.5 3.1 %reshape.53 = f32[640,2,256]{2,1,0:T(2,128)} reshape(f32[640,512]{1,0:T(8,128)} %get-tuple-element.24) | data formatting | bytes 2621440 | tf_op jit(solution)/shard_map/reshape | solution.py:516
  240.5 0.0 copy-done.1
  240.5 0.0 copy-start
  240.6 1.5 copy.15
  242.0 1.2 copy-done
  243.2 1.5 copy.16
Async XLA Ops:
  237.4 3.1 %copy-start.1 = (bf16[512,2560]{1,0:T(8,128)(2,1)S(1)}, bf16[512,2560]{1,0:T(8,128)(2,1)}, u32[]{:S(2)}) copy-start(bf16[512,2560]{1,0:T(8,128)(2,1)} %get-tuple-element.22) | copy-start | bytes 7864324
  240.5 2.7 %copy-start = (bf16[512,2560]{1,0:T(8,128)(2,1)S(1)}, bf16[512,2560]{1,0:T(8,128)(2,1)}, u32[]{:S(2)}) copy-start(bf16[512,2560]{1,0:T(8,128)(2,1)} %get-tuple-element.23) | copy-start | bytes 7864324

commit v3 on v2

v3 whole, which is shorter than its diff:
```python
import functools

import jax
import jax.numpy as jnp
from jax import lax
from jax.experimental import pallas as pl
from jax.experimental.pallas import tpu as pltpu
from jax.sharding import PartitionSpec as P

HEAD_DIM = 128
MESH = pl.DeviceIdType.MESH
F32 = jnp.float32
BF16 = jnp.bfloat16
VMEM_LIMIT = 60 * 1024 * 1024
NT = (((1,), (1,)), ((), ()))
TN = (((0,), (0,)), ((), ()))
EXTRA = 16
STEPS = 32000.0


def place_of(index, n):
    side = index % 2
    row = index // 2
    return row + side * (n - 1 - 2 * row)


def index_at(place, n):
    place = (place + 2 * n) % n
    back = place // (n // 2)
    return 2 * (place + back * (n - 1 - 2 * place)) + back


def enter(peers):
    barrier = pltpu.get_barrier_semaphore()
    for peer in peers:
        pl.semaphore_signal(barrier, inc=1, device_id=peer, device_id_type=MESH)
    pl.semaphore_wait(barrier, len(peers))


class Ring:
    def __init__(self, buf, send, recv, n):
        self.buf, self.send, self.recv, self.n = buf, send, recv, n
        self.place = place_of(lax.axis_index("dp"), n)
        self.copies = []

    def owner(self, way, step):
        return index_at(self.place - step if way == 0 else self.place + step, self.n)

    def pieces(self, way, step):
        if step < self.n // 2 - 1:
            return (0, 1) if way == 0 else (1, 0)
        return (way,)

    def copy(self, way, step, piece):
        to = index_at(self.place + 1 if way == 0 else self.place - 1, self.n)
        block = self.buf.at[2 * self.owner(way, step) + piece]
        return pltpu.make_async_remote_copy(
            src_ref=block,
            dst_ref=block,
            send_sem=self.send.at[way, step, piece],
            recv_sem=self.recv.at[way, step, piece],
            device_id={"dp": to},
            device_id_type=MESH,
        )

    def landed(self, way, step, piece):
        block = self.buf.at[2 * self.owner(way, step + 1) + piece]
        pltpu.make_async_remote_copy(
            src_ref=block,
            dst_ref=block,
            send_sem=self.send.at[way, step, piece],
            recv_sem=self.recv.at[way, step, piece],
            device_id={"dp": self.owner(1, 1)},
            device_id_type=MESH,
        ).wait_recv()

    def run(self, use):
        last = self.n // 2
        for step in range(last + 1):
            for order in range(2):
                for way in range(2):
                    if step > 0:
                        came = self.pieces(way, step - 1)
                        if order < len(came):
                            self.landed(way, step - 1, came[order])
                    if step < last:
                        going = self.pieces(way, step)
                        if order < len(going):
                            copy = self.copy(way, step, going[order])
                            copy.start()
                            self.copies.append(copy)
            if step == 0 or step == last:
                use([self.owner(0, step)], step)
            else:
                use([self.owner(0, step), self.owner(1, step)], step)

    def finish(self):
        for copy in self.copies:
            copy.wait_send()


def attend_one(c, k, group, length, kp, vp, ko, vo, q, cot, att, gq):
    slots = ko.shape[0]
    scale = HEAD_DIM ** (-0.5)
    live = lax.broadcasted_iota(jnp.int32, (slots, HEAD_DIM), 0) < length
    cols = group * slots
    key_id = lax.broadcasted_iota(jnp.int32, (slots, cols), 0)
    row_id = lax.broadcasted_iota(jnp.int32, (slots, cols), 1) % slots
    allowed = key_id <= row_id
    heads = [slice((k * group + g) * HEAD_DIM, (k * group + g + 1) * HEAD_DIM) for g in range(group)]
    qk = jnp.concatenate([q[c, :, h] for h in heads], axis=0)
    do = jnp.concatenate([jnp.where(live, cot[c, :, h].astype(F32), 0.0).astype(BF16) for h in heads], axis=0)
    sp = lax.dot_general(kp, qk, NT, preferred_element_type=F32)
    so = lax.dot_general(ko, qk, NT, preferred_element_type=F32)
    so = jnp.where(allowed, so, -1e30)
    top = jnp.maximum(jnp.max(sp, axis=0, keepdims=True), jnp.max(so, axis=0, keepdims=True))
    ep = jnp.exp((sp - top) * scale)
    eo = jnp.exp((so - top) * scale)
    inv = 1.0 / (jnp.sum(ep, axis=0, keepdims=True) + jnp.sum(eo, axis=0, keepdims=True))
    pp = ep * inv
    po = eo * inv
    wp = pp.astype(BF16)
    wo = po.astype(BF16)
    dp = lax.dot_general(vp, do, NT, preferred_element_type=F32)
    dn = lax.dot_general(vo, do, NT, preferred_element_type=F32)
    delta = jnp.sum(pp * dp, axis=0, keepdims=True) + jnp.sum(po * dn, axis=0, keepdims=True)
    gp = (pp * (dp - delta) * scale).astype(BF16)
    go = (po * (dn - delta) * scale).astype(BF16)
    mixed = lax.dot_general(vp, wp, TN, preferred_element_type=F32) + lax.dot_general(
        vo, wo, TN, preferred_element_type=F32
    )
    dq = lax.dot_general(kp, gp, TN, preferred_element_type=F32) + lax.dot_general(
        ko, go, TN, preferred_element_type=F32
    )
    mixed = mixed.T
    dq = dq.T
    for g, h in enumerate(heads):
        rows = slice(g * slots, (g + 1) * slots)
        att[c, :, h] = jnp.where(live, mixed[rows], 0.0).astype(BF16)
        gq[c, :, h] = dq[rows].astype(BF16)
    return (
        jnp.dot(gp, qk, preferred_element_type=F32).astype(BF16),
        jnp.dot(wp, do, preferred_element_type=F32).astype(BF16),
        jnp.dot(go, qk, preferred_element_type=F32).astype(BF16),
        jnp.dot(wo, do, preferred_element_type=F32).astype(BF16),
    )


def layer_kernel(
    n, per, kv_heads, prompt_of, which, marks, lens, w_ref, ph_hbm, oh_hbm, q_hbm, cot_hbm,
    att_hbm, gq_hbm, wall_hbm, g_ref, *scratch,
):
    ph_ref, oh_ref, q, cot, att, gq, wall_ref, acc, own_kv = scratch[:9]
    pkv, terms, leave, got = (scratch[9 + i * kv_heads : 9 + (i + 1) * kv_heads] for i in range(4))
    load, store, here, send_w, recv_w, send_k, recv_k, send_t, recv_t = scratch[9 + 4 * kv_heads :]
    me = lax.axis_index("dp")
    place = place_of(me, n)
    depth = w_ref.shape[0]
    rows = ph_ref.shape[0]
    plen = rows // per
    comps, slots, features = q.shape
    width = w_ref.shape[1] // 2
    group = features // HEAD_DIM // kv_heads
    tile = min(256, rows)
    last = n // 2
    loads = [
        pltpu.make_async_copy(src, dst, load.at[i])
        for i, (src, dst) in enumerate(((ph_hbm, ph_ref), (oh_hbm, oh_ref), (q_hbm, q), (cot_hbm, cot)))
    ]
    for one in loads:
        one.start()
    wall_ref[2 * me] = w_ref[: depth // 2]
    wall_ref[2 * me + 1] = w_ref[depth // 2 :]
    peers = [index_at(place + d, n) for d in range(1, n)]
    enter([{"dp": peer} for peer in peers])
    ring = Ring(wall_ref, send_w, recv_w, n)

    def add(owners, step):
        if step == 0:
            for one in loads:
                one.wait()
        for source, base in ((ph_ref, 0), (oh_ref, rows)):

            @pl.loop(0, rows // tile)
            def _(r):
                at = pl.multiple_of(r * tile, tile)
                total = None
                for owner in owners:
                    cols = pl.ds(pl.multiple_of(owner * depth, 128), depth)
                    term = jnp.dot(
                        source[pl.ds(at, tile), cols],
                        wall_ref[pl.ds(2 * owner, 2)].reshape(depth, 2 * width),
                        preferred_element_type=F32,
                    )
                    total = term if total is None else total + term
                to = pl.ds(base + at, tile)
                if step == 0:
                    acc[to] = total
                else:
                    acc[to] += total

    ring.run(add)
    wall_out = pltpu.make_async_copy(wall_ref, wall_hbm, store.at[0])
    wall_out.start()

    def head_cols(k):
        return slice(k * HEAD_DIM, (k + 1) * HEAD_DIM), slice(width + k * HEAD_DIM, width + (k + 1) * HEAD_DIM)

    for k in range(kv_heads):
        ks, vs = head_cols(k)
        for s in range(per):
            pkv[k][per * me + s, :, :HEAD_DIM] = acc[s * plen : (s + 1) * plen, ks].astype(BF16)
            pkv[k][per * me + s, :, HEAD_DIM:] = acc[s * plen : (s + 1) * plen, vs].astype(BF16)

    def attend(k, first, count):
        ks, vs = head_cols(k)

        @pl.loop(first, first + count)
        def _(c):
            both = pkv[k][prompt_of[c]]
            own = pl.ds(pl.multiple_of(c * slots, slots), slots)
            tk, tv, ok, ov = attend_one(
                c, k, group, lens[c], both[:, :HEAD_DIM], both[:, HEAD_DIM:],
                own_kv[own, ks], own_kv[own, vs], q, cot, att, gq,
            )
            terms[k][c, :, :HEAD_DIM] = tk
            terms[k][c, :, HEAD_DIM:] = tv
            low = pl.ds(pl.multiple_of(rows + c * slots, slots), slots)
            g_ref[low, ks] = ok
            g_ref[low, vs] = ov

    def ready(k):
        for e in range(n):
            leave[k][e, :plen] = terms[k][which[e]]
            leave[k][e, plen:] = jnp.full((EXTRA, 2 * HEAD_DIM), marks[e].astype(F32), F32).astype(BF16)

    order = sorted(range(1, n), key=lambda d: -min(d, n - d))
    swaps = []

    def swap(k):
        for d in order:
            peer = peers[d - 1]
            one = pltpu.make_async_remote_copy(
                src_ref=leave[k].at[peer],
                dst_ref=got[k].at[me],
                send_sem=send_t.at[k, d],
                recv_sem=recv_t.at[k, d],
                device_id={"dp": peer},
                device_id_type=MESH,
            )
            one.start()
            swaps.append(one)

    def collect(k):
        own_copy = pltpu.make_async_copy(leave[k].at[me], got[k].at[me], here)
        own_copy.start()
        own_copy.wait()
        for d in order:
            came = got[k].at[index_at(place - d, n)]
            pltpu.make_async_remote_copy(
                src_ref=came,
                dst_ref=came,
                send_sem=send_t.at[k, d],
                recv_sem=recv_t.at[k, d],
                device_id={"dp": peers[0]},
                device_id_type=MESH,
            ).wait_recv()
        ks, vs = head_cols(k)
        for s in range(per):
            total = jnp.zeros((plen, 2 * HEAD_DIM), F32)
            for e in range(n):
                mark = got[k][e, plen:].astype(F32)[:1]
                total = total + jnp.where(mark == float(s + 1), got[k][e, :plen].astype(F32), 0.0)
            kept = total.astype(BF16)
            g_ref[s * plen : (s + 1) * plen, ks] = kept[:, :HEAD_DIM]
            g_ref[s * plen : (s + 1) * plen, vs] = kept[:, HEAD_DIM:]

    def own_rows(owners, step):
        if step == 0:
            own_kv[...] = acc[rows:].astype(BF16)

    rings = [Ring(pkv[k], send_k.at[k], recv_k.at[k], n) for k in range(kv_heads)]
    share = -(-comps // last)
    for k in range(kv_heads):

        def beside(owners, step, k=k):
            if k == 0:
                own_rows(owners, step)
            elif step < last and step * share < comps:
                attend(k - 1, step * share, min(share, comps - step * share))

        rings[k].run(beside)
        if k > 0:
            ready(k - 1)
            swap(k - 1)
    attend(kv_heads - 1, 0, comps)
    ready(kv_heads - 1)
    swap(kv_heads - 1)
    outs = [pltpu.make_async_copy(att, att_hbm, store.at[1]), pltpu.make_async_copy(gq, gq_hbm, store.at[2])]
    for one in outs:
        one.start()
    for k in range(kv_heads):
        collect(k)
    wall_out.wait()
    for one in outs:
        one.wait()
    for one in [ring] + rings:
        one.finish()
    for one in swaps:
        one.wait_send()


def layer(prompt_of, lens, w, ph, oh, q, cot, n, per):
    depth, width = w.shape
    rows = ph.shape[0]
    plen = rows // per
    comps = q.shape[0]
    kv_heads = width // (2 * HEAD_DIM)
    hold = 2 * HEAD_DIM
    fits = prompt_of[None, :] // per == jnp.arange(n, dtype=jnp.int32)[:, None]
    which = jnp.sum(jnp.where(fits, jnp.arange(comps, dtype=jnp.int32)[None, :], 0), axis=1)
    marks = jnp.sum(jnp.where(fits, prompt_of[None, :] % per + 1, 0), axis=1)
    vmem = pl.BlockSpec(memory_space=pltpu.VMEM)
    hbm = pl.BlockSpec(memory_space=pl.ANY)
    smem = pl.BlockSpec(memory_space=pltpu.SMEM)
    wide = pltpu.VMEM(q.shape, BF16)
    sems = pltpu.SemaphoreType.DMA((2, n // 2, 2))
    more = pltpu.SemaphoreType.DMA((kv_heads, 2, n // 2, 2))
    swap_sems = pltpu.SemaphoreType.DMA((kv_heads, n))
    return pl.pallas_call(
        functools.partial(layer_kernel, n, per, kv_heads),
        out_shape=(
            jax.ShapeDtypeStruct(q.shape, BF16),
            jax.ShapeDtypeStruct(q.shape, BF16),
            jax.ShapeDtypeStruct((2 * n, depth // 2, width), BF16),
            jax.ShapeDtypeStruct((rows + oh.shape[0], width), BF16),
        ),
        in_specs=[smem] * 4 + [vmem] + [hbm] * 4,
        out_specs=(hbm, hbm, hbm, vmem),
        scratch_shapes=[
            pltpu.VMEM(ph.shape, BF16),
            pltpu.VMEM(oh.shape, BF16),
            wide,
            wide,
            wide,
            wide,
            pltpu.VMEM((2 * n, depth // 2, width), BF16),
            pltpu.VMEM((rows + oh.shape[0], width), F32),
            pltpu.VMEM((oh.shape[0], width), BF16),
        ]
        + [pltpu.VMEM((n * per, plen, hold), BF16)] * kv_heads
        + [pltpu.VMEM((comps, plen, hold), BF16)] * kv_heads
        + [pltpu.VMEM((n, plen + EXTRA, hold), BF16)] * (2 * kv_heads)
        + [
            pltpu.SemaphoreType.DMA((4,)),
            pltpu.SemaphoreType.DMA((3,)),
            pltpu.SemaphoreType.DMA,
            sems,
            sems,
            more,
            more,
            swap_sems,
            swap_sems,
        ],
        compiler_params=pltpu.CompilerParams(collective_id=0, has_side_effects=True, vmem_limit_bytes=VMEM_LIMIT),
        name="layer",
    )(prompt_of, which, marks, lens, w, ph, oh, q, cot)


def encode(block, ref):
    top = jnp.maximum(jnp.max(jnp.abs(block), axis=0, keepdims=True), 1e-30)
    power = jnp.ceil(jnp.log2(top))
    rows = block.shape[0]
    ref[:rows] = jnp.round(block * (jnp.exp2(-power) * STEPS)).astype(jnp.int32).astype(jnp.int16)
    ref[rows:] = jnp.broadcast_to(power, (EXTRA, block.shape[1])).astype(jnp.int32).astype(jnp.int16)


def decode(ref):
    rows = ref.shape[0] - EXTRA
    power = ref[rows:].astype(jnp.int32).astype(F32)[:1]
    return ref[:rows].astype(jnp.int32).astype(F32) * (jnp.exp2(power) * (1.0 / STEPS))


def grads_kernel(
    n, chunk, g_ref, ph_hbm, oh_hbm, wall_hbm, fp_ref, fo_ref, gw_ref,
    gt_ref, ph_ref, oh_ref, wall_ref, slots, fsend, frecv, load, send, recv, send_f, recv_f,
):
    me = lax.axis_index("dp")
    mp = lax.axis_index("mp")
    place = place_of(me, n)
    right = index_at(place + 1, n)
    left = index_at(place - 1, n)
    other = {"mp": 1 - mp}
    rows = ph_ref.shape[0]
    depth = gw_ref.shape[0]
    width = gt_ref.shape[0]
    half = width // 2
    last = n // 2
    chunks = fsend.shape[1]
    tile = min(256, rows)
    loads = [
        pltpu.make_async_copy(src, dst, load.at[i])
        for i, (src, dst) in enumerate(((oh_hbm, oh_ref), (ph_hbm, ph_ref), (wall_hbm, wall_ref)))
    ]
    for one in loads:
        one.start()
    enter([{"dp": right}, {"dp": left}, other])
    span = chunk * chunks

    def product(first, at):
        return lax.dot_general(
            g_ref[pl.ds(at, tile)], wall_ref[pl.ds(first, chunk)], NT, preferred_element_type=F32
        ).astype(BF16)

    feature = {}

    def away(part):
        for j in range(chunks):
            first = pl.multiple_of((1 - mp) * span + j * chunk, 128)

            @pl.loop(0, rows // tile)
            def _(r):
                at = pl.multiple_of(r * tile, tile)
                fsend[part, j, pl.ds(at, tile)] = product(first, pl.multiple_of(part * rows + at, tile))

            one = pltpu.make_async_remote_copy(
                src_ref=fsend.at[part, j],
                dst_ref=frecv.at[part, j],
                send_sem=send_f.at[part, j],
                recv_sem=recv_f.at[part, j],
                device_id=other,
                device_id_type=MESH,
            )
            one.start()
            feature[part, j] = one

    def home(part, out_ref):
        for j in range(chunks):
            first = pl.multiple_of(mp * span + j * chunk, 128)
            feature[part, j].wait_recv()

            @pl.loop(0, rows // tile)
            def _(r):
                at = pl.multiple_of(r * tile, tile)
                mine = product(first, pl.multiple_of(part * rows + at, tile)).astype(F32)
                total = mine + frecv[part, j, pl.ds(at, tile)].astype(F32)
                out_ref[pl.ds(at, tile), j * chunk : (j + 1) * chunk] = total.astype(BF16)

    for lane in range(0, width, half):
        gt_ref[lane : lane + half] = g_ref[:, lane : lane + half].astype(F32).T.astype(BF16)
    loads[0].wait()
    loads[1].wait()

    def partial(target, piece):
        cols = pl.ds(pl.multiple_of(target * depth, 128), depth)
        top = gt_ref[piece * half : (piece + 1) * half]
        return jnp.dot(top[:, :rows], ph_ref[:, cols], preferred_element_type=F32) + jnp.dot(
            top[:, rows:], oh_ref[:, cols], preferred_element_type=F32
        )

    def copy(way, step, piece):
        return pltpu.make_async_remote_copy(
            src_ref=slots.at[way, step, piece],
            dst_ref=slots.at[way, step + 1, piece],
            send_sem=send.at[way, step, piece],
            recv_sem=recv.at[way, step, piece],
            device_id={"dp": right if way == 0 else left},
            device_id_type=MESH,
        )

    started = []

    def go(way, step, piece):
        one = copy(way, step, piece)
        one.start()
        started.append(one)

    far = index_at(place + last, n)
    for way in range(2):
        encode(partial(far, way), slots.at[way, 0, way])
        go(way, 0, way)
    for way in range(2):
        near = index_at(place + (last - 1) if way == 0 else place - (last - 1), n)
        encode(partial(near, 1 - way), slots.at[way, 1, 1 - way])
        go(way, 1, 1 - way)
    loads[2].wait()
    away(0)
    away(1)
    for step in range(1, last):
        for turn in range(2):
            for way in range(2):
                piece = way if turn == 0 else 1 - way
                if step == 1 and piece != way:
                    continue
                target = index_at(place + (last - step) if way == 0 else place - (last - step), n)
                mine = partial(target, piece)
                copy(way, step - 1, piece).wait_recv()
                encode(decode(slots.at[way, step, piece]) + mine, slots.at[way, step, piece])
                go(way, step, piece)
        if step == 1:
            home(0, fp_ref)
        if step == min(2, last - 1):
            home(1, fo_ref)
    for piece in range(2):
        mine = partial(me, piece)
        for way in range(2):
            copy(way, last - 1, piece).wait_recv()
        total = mine + decode(slots.at[0, last, piece]) + decode(slots.at[1, last, piece])
        gw_ref[:, piece * half : (piece + 1) * half] = total.T
    for one in started + list(feature.values()):
        one.wait_send()


def grads(g, ph, oh, wall, n, n_mp):
    rows, model_dim = ph.shape
    width = g.shape[1]
    depth = model_dim // n
    share = model_dim // n_mp
    chunk = 512 if share % 512 == 0 else 128
    chunks = share // chunk
    vmem = pl.BlockSpec(memory_space=pltpu.VMEM)
    hbm = pl.BlockSpec(memory_space=pl.ANY)
    sems = pltpu.SemaphoreType.DMA((2, n // 2, 2))
    return pl.pallas_call(
        functools.partial(grads_kernel, n, chunk),
        out_shape=(
            jax.ShapeDtypeStruct((rows, share), BF16),
            jax.ShapeDtypeStruct((rows, share), BF16),
            jax.ShapeDtypeStruct((depth, width), F32),
        ),
        in_specs=[vmem, hbm, hbm, hbm],
        out_specs=(vmem,) * 3,
        scratch_shapes=[
            pltpu.VMEM((width, 2 * rows), BF16),
            pltpu.VMEM(ph.shape, BF16),
            pltpu.VMEM(oh.shape, BF16),
            pltpu.VMEM(wall.shape, BF16),
            pltpu.VMEM((2, n // 2 + 1, 2, width // 2 + EXTRA, depth), jnp.int16),
            pltpu.VMEM((2, chunks, rows, chunk), BF16),
            pltpu.VMEM((2, chunks, rows, chunk), BF16),
            pltpu.SemaphoreType.DMA((3,)),
            sems,
            sems,
            pltpu.SemaphoreType.DMA((2, chunks)),
            pltpu.SemaphoreType.DMA((2, chunks)),
        ],
        compiler_params=pltpu.CompilerParams(collective_id=2, has_side_effects=True, vmem_limit_bytes=VMEM_LIMIT),
        name="grads_reduce",
    )(g, ph, oh, wall)


def shards(n, n_mp, prompt_hidden, completion_hidden, queries, cotangent, kv_weight, prompt_of, comp_len):
    per, plen, model_dim = prompt_hidden.shape
    comps, slots, _ = completion_hidden.shape
    depth, _, kv_width = kv_weight.shape
    width = 2 * kv_width
    w = kv_weight.reshape(depth, width)
    ph = prompt_hidden.reshape(per * plen, model_dim)
    oh = completion_hidden.reshape(comps * slots, model_dim)
    attended, grad_queries, wall, g = layer(
        prompt_of, comp_len.reshape(-1), w, ph, oh, queries, cotangent, n, per
    )
    fp, fo, gw = grads(g, ph, oh, wall.reshape(model_dim, width), n, n_mp)
    return (
        attended,
        grad_queries,
        fp.reshape(per, plen, -1),
        fo.reshape(comps, slots, -1),
        gw.reshape(depth, 2, kv_width),
    )


def solution(mesh):
    in_specs = (
        P(("groups", "dp"), None, None),
        P(("groups", "dp"), None, None),
        P(("groups", "dp"), None, "mp"),
        P(("groups", "dp"), None, "mp"),
        P("dp", None, "mp"),
        P(("groups", "dp")),
        P(("groups", "dp"), None),
    )
    out_specs = (P(("groups", "dp"), None, "mp"),) * 5
    body = functools.partial(shards, mesh.shape["dp"], mesh.shape["mp"])
    return jax.shard_map(body, mesh=mesh, in_specs=in_specs, out_specs=out_specs, check_vma=False)
```

time: 245 us -> 229 us (0.935)
  Pallas kernels: 235 us -> 213 us
  local copies, waits for them, and re-layouts: 9.31 us -> 14.1 us
    pallas_call x3 -> x2, Pallas kernels: 235 us -> 213 us  [the longest x1 150 us: layer(): pl.pallas_call(functools.partial(layer_kernel, n, per, kv_heads), out_sha...]
    unnamed x7 -> x13, local copies, waits for them, and re-layouts: 6.21 us -> 11.1 us
where the time goes in v3:
time: 229 us
  Pallas kernels  213 us (93%)
  local copies, waits for them, and re-layouts  14.1 us (6%)
    pallas_call x1, Pallas kernels, layer(): pl.pallas_call(functools.partial(layer_kernel, n, per, kv_heads), out_sha...  150 us
    pallas_call x1, Pallas kernels, grads(): pl.pallas_call(functools.partial(grads_kernel, n, chunk), out_shape=(jax....  62.7 us
    unnamed x13, local copies, waits for them, and re-layouts  11.1 us

profile of v3, /device:TPU:0, one launch (start us, length us, event | category | flops | bytes accessed | tf_op | source)
XLA Modules:
  0.0 228.9 jit_solution(6143358591227043064)
XLA Ops:
  0.6 0.7 and_select_fusion.1
  1.3 0.7 select_reduce_fusion
  2.0 2.0 copy.12
  4.0 150.1 %layer.1 = (bf16[8,64,2048]{2,1,0:T(8,128)(2,1)}, bf16[8,64,2048]{2,1,0:T(8,128)(2,1)}, bf16[16,320,512]{2,1,0:T(8,128)(2,1)}, bf16[1024,512]{1,0:T(8,128)(2,1)}) custom-call(s32[8]{0:T(128)} %prompt_of.1, s32[8]{0:T(128)} %get-tuple-element.20.which, s32[8]{0:T(128)} %get-tuple-element.19.marks, s32[8]{0:T(128)} %bitcast.17, bf16[640,512]{1,0:T(8,128)(2,1)} %bitcast.13, ...), custom_call_target="tpu_custom_call" | custom-call | tf_op jit(solution)/shard_map/layer/pallas_call | solution.py:330
  154.1 62.7 %grads_reduce.1 = (bf16[512,2560]{1,0:T(8,128)(2,1)}, bf16[512,2560]{1,0:T(8,128)(2,1)}, f32[640,512]{1,0:T(8,128)}) custom-call(bf16[1024,512]{1,0:T(8,128)(2,1)} %get-tuple-element.14.g_ref, bf16[512,5120]{1,0:T(8,128)(2,1)} %bitcast.9, bf16[512,5120]{1,0:T(8,128)(2,1)} %bitcast.11, bf16[5120,512]{1,0:T(8,128)(2,1)} %bitcast.12), custom_call_target="tpu_custom_call" | custom-call | tf_op jit(solution)/shard_map/grads_reduce/pallas_call | solution.py:524
  216.8 0.0 copy-start.3
  216.8 3.1 %reshape.68 = f32[640,2,256]{2,1,0:T(2,128)} reshape(f32[640,512]{1,0:T(8,128)} %get-tuple-element.18) | data formatting | bytes 2621440 | tf_op jit(solution)/shard_map/reshape | solution.py:569
  219.9 0.0 copy-done.3
  219.9 0.0 copy-start.2
  219.9 1.3 copy.17
  221.2 1.0 copy-done.2
  222.2 0.0 copy-start.1
  222.2 1.3 copy.18
  223.6 1.2 copy-done.1
  224.7 0.0 copy-start
  224.7 1.5 copy.19
  226.2 1.2 copy-done
  227.4 1.5 copy.20
Async XLA Ops:
  216.8 3.1 %copy-start.3 = (bf16[8,64,2048]{2,1,0:T(8,128)(2,1)S(1)}, bf16[8,64,2048]{2,1,0:T(8,128)(2,1)}, u32[]{:S(2)}) copy-start(bf16[8,64,2048]{2,1,0:T(8,128)(2,1)} %get-tuple-element.28) | copy-start | bytes 6291460
  219.9 2.3 %copy-start.2 = (bf16[8,64,2048]{2,1,0:T(8,128)(2,1)S(1)}, bf16[8,64,2048]{2,1,0:T(8,128)(2,1)}, u32[]{:S(2)}) copy-start(bf16[8,64,2048]{2,1,0:T(8,128)(2,1)} %get-tuple-element.29) | copy-start | bytes 6291460
  222.2 2.5 %copy-start.1 = (bf16[512,2560]{1,0:T(8,128)(2,1)S(1)}, bf16[512,2560]{1,0:T(8,128)(2,1)}, u32[]{:S(2)}) copy-start(bf16[512,2560]{1,0:T(8,128)(2,1)} %get-tuple-element.16) | copy-start | bytes 7864324
  224.7 2.7 %copy-start = (bf16[512,2560]{1,0:T(8,128)(2,1)S(1)}, bf16[512,2560]{1,0:T(8,128)(2,1)}, u32[]{:S(2)}) copy-start(bf16[512,2560]{1,0:T(8,128)(2,1)} %get-tuple-element.17) | copy-start | bytes 7864324

commit v4 on v3

--- a/solution.py
+++ b/solution.py
@@ -38,8 +38,8 @@
 
 
 class Ring:
-    def __init__(self, buf, send, recv, n):
-        self.buf, self.send, self.recv, self.n = buf, send, recv, n
+    def __init__(self, block, send, recv, n):
+        self.block, self.send, self.recv, self.n = block, send, recv, n
         self.place = place_of(lax.axis_index("dp"), n)
         self.copies = []
 
@@ -53,7 +53,7 @@
 
     def copy(self, way, step, piece):
         to = index_at(self.place + 1 if way == 0 else self.place - 1, self.n)
-        block = self.buf.at[2 * self.owner(way, step) + piece]
+        block = self.block(self.owner(way, step), piece)
         return pltpu.make_async_remote_copy(
             src_ref=block,
             dst_ref=block,
@@ -64,7 +64,7 @@
         )
 
     def landed(self, way, step, piece):
-        block = self.buf.at[2 * self.owner(way, step + 1) + piece]
+        block = self.block(self.owner(way, step + 1), piece)
         pltpu.make_async_remote_copy(
             src_ref=block,
             dst_ref=block,
@@ -152,7 +152,7 @@
 ):
     ph_ref, oh_ref, q, cot, att, gq, wall_ref, acc, own_kv = scratch[:9]
     pkv, terms, leave, got = (scratch[9 + i * kv_heads : 9 + (i + 1) * kv_heads] for i in range(4))
-    load, store, here, send_w, recv_w, send_k, recv_k, send_t, recv_t = scratch[9 + 4 * kv_heads :]
+    load, store, here, send_w, recv_w, send_x, recv_x, send_k, recv_k, send_t, recv_t = scratch[9 + 4 * kv_heads :]
     me = lax.axis_index("dp")
     place = place_of(me, n)
     depth = w_ref.shape[0]
@@ -169,11 +169,40 @@
     ]
     for one in loads:
         one.start()
-    wall_ref[2 * me] = w_ref[: depth // 2]
-    wall_ref[2 * me + 1] = w_ref[depth // 2 :]
+    wall_ref[me] = w_ref[...]
     peers = [index_at(place + d, n) for d in range(1, n)]
-    enter([{"dp": peer} for peer in peers])
-    ring = Ring(wall_ref, send_w, recv_w, n)
+    group_id = lax.axis_index("groups")
+    side = group_id % 2
+    twin = {"groups": group_id + 1 - 2 * side}
+    enter([{"dp": peer} for peer in peers] + [twin])
+    skip = depth * 3 // 10 // 32 * 32
+    piece_rows = (depth - skip) // 2
+    ring = Ring(
+        lambda owner, piece: wall_ref.at[owner, pl.ds(pl.multiple_of(side * skip + piece * piece_rows, 16), piece_rows)],
+        send_w, recv_w, n,
+    )
+
+    def across(owner, way, step):
+        rows_out = pl.ds(pl.multiple_of(side * (depth - skip), 16), skip)
+        return pltpu.make_async_remote_copy(
+            src_ref=wall_ref.at[owner, rows_out],
+            dst_ref=wall_ref.at[owner, rows_out],
+            send_sem=send_x.at[way, step],
+            recv_sem=recv_x.at[way, step],
+            device_id=twin,
+            device_id_type=MESH,
+        )
+
+    def crossed(owner, way, step):
+        rows_in = wall_ref.at[owner, pl.ds(pl.multiple_of((1 - side) * (depth - skip), 16), skip)]
+        pltpu.make_async_remote_copy(
+            src_ref=rows_in,
+            dst_ref=rows_in,
+            send_sem=send_x.at[way, step],
+            recv_sem=recv_x.at[way, step],
+            device_id=twin,
+            device_id_type=MESH,
+        ).wait_recv()
 
     def add(owners, step):
         if step == 0:
@@ -189,7 +218,7 @@
                     cols = pl.ds(pl.multiple_of(owner * depth, 128), depth)
                     term = jnp.dot(
                         source[pl.ds(at, tile), cols],
-                        wall_ref[pl.ds(2 * owner, 2)].reshape(depth, 2 * width),
+                        wall_ref[owner],
                         preferred_element_type=F32,
                     )
                     total = term if total is None else total + term
@@ -199,7 +228,28 @@
                 else:
                     acc[to] += total
 
-    ring.run(add)
+    pending, crossing = [], []
+
+    def finish_pending():
+        if pending:
+            owners, step = pending.pop()
+            for way, owner in enumerate(owners):
+                crossed(owner, way, step)
+            add(owners, step)
+
+    def gathered(owners, step):
+        if step == 0:
+            add(owners, step)
+            return
+        for way, owner in enumerate(owners):
+            one = across(owner, way, step)
+            one.start()
+            crossing.append(one)
+        finish_pending()
+        pending.append((owners, step))
+
+    ring.run(gathered)
+    finish_pending()
     wall_out = pltpu.make_async_copy(wall_ref, wall_hbm, store.at[0])
     wall_out.start()
 
@@ -279,7 +329,10 @@
         if step == 0:
             own_kv[...] = acc[rows:].astype(BF16)
 
-    rings = [Ring(pkv[k], send_k.at[k], recv_k.at[k], n) for k in range(kv_heads)]
+    rings = [
+        Ring(lambda owner, piece, k=k: pkv[k].at[2 * owner + piece], send_k.at[k], recv_k.at[k], n)
+        for k in range(kv_heads)
+    ]
     share = -(-comps // last)
     for k in range(kv_heads):
 
@@ -306,7 +359,7 @@
         one.wait()
     for one in [ring] + rings:
         one.finish()
-    for one in swaps:
+    for one in swaps + crossing:
         one.wait_send()
 
 
@@ -332,7 +385,7 @@
         out_shape=(
             jax.ShapeDtypeStruct(q.shape, BF16),
             jax.ShapeDtypeStruct(q.shape, BF16),
-            jax.ShapeDtypeStruct((2 * n, depth // 2, width), BF16),
+            jax.ShapeDtypeStruct((n, depth, width), BF16),
             jax.ShapeDtypeStruct((rows + oh.shape[0], width), BF16),
         ),
         in_specs=[smem] * 4 + [vmem] + [hbm] * 4,
@@ -344,7 +397,7 @@
             wide,
             wide,
             wide,
-            pltpu.VMEM((2 * n, depth // 2, width), BF16),
+            pltpu.VMEM((n, depth, width), BF16),
             pltpu.VMEM((rows + oh.shape[0], width), F32),
             pltpu.VMEM((oh.shape[0], width), BF16),
         ]
@@ -357,6 +410,8 @@
             pltpu.SemaphoreType.DMA,
             sems,
             sems,
+            pltpu.SemaphoreType.DMA((2, n // 2 + 1)),
+            pltpu.SemaphoreType.DMA((2, n // 2 + 1)),
             more,
             more,
             swap_sems,

time: 229 us -> 222 us (0.969)
  Pallas kernels: 213 us -> 206 us
    pallas_call x1, Pallas kernels: 150 us -> 143 us  [layer(): pl.pallas_call(functools.partial(layer_kernel, n, per, kv_heads), out_sha...]
where the time goes in v4:
time: 222 us
  Pallas kernels  206 us (93%)
  local copies, waits for them, and re-layouts  14.1 us (6%)
    pallas_call x1, Pallas kernels, layer(): pl.pallas_call(functools.partial(layer_kernel, n, per, kv_heads), out_sha...  143 us
    pallas_call x1, Pallas kernels, grads(): pl.pallas_call(functools.partial(grads_kernel, n, chunk), out_shape=(jax....  62.6 us
    unnamed x13, local copies, waits for them, and re-layouts  11.1 us

profile of v4, /device:TPU:0, one launch (start us, length us, event | category | flops | bytes accessed | tf_op | source)
XLA Modules:
  0.0 221.7 jit_solution(10314526608592150220)
XLA Ops:
  0.6 0.7 and_select_fusion.1
  1.3 0.7 select_reduce_fusion
  2.0 2.0 copy.12
  4.0 143.0 %layer.1 = (bf16[8,64,2048]{2,1,0:T(8,128)(2,1)}, bf16[8,64,2048]{2,1,0:T(8,128)(2,1)}, bf16[8,640,512]{2,1,0:T(8,128)(2,1)}, bf16[1024,512]{1,0:T(8,128)(2,1)}) custom-call(s32[8]{0:T(128)} %prompt_of.1, s32[8]{0:T(128)} %get-tuple-element.20.which, s32[8]{0:T(128)} %get-tuple-element.19.marks, s32[8]{0:T(128)} %bitcast.17, bf16[640,512]{1,0:T(8,128)(2,1)} %bitcast.13, ...), custom_call_target="tpu_custom_call" | custom-call | tf_op jit(solution)/shard_map/layer/pallas_call | solution.py:383
  147.0 62.6 %grads_reduce.1 = (bf16[512,2560]{1,0:T(8,128)(2,1)}, bf16[512,2560]{1,0:T(8,128)(2,1)}, f32[640,512]{1,0:T(8,128)}) custom-call(bf16[1024,512]{1,0:T(8,128)(2,1)} %get-tuple-element.14.g_ref, bf16[512,5120]{1,0:T(8,128)(2,1)} %bitcast.9, bf16[512,5120]{1,0:T(8,128)(2,1)} %bitcast.11, bf16[5120,512]{1,0:T(8,128)(2,1)} %bitcast.12), custom_call_target="tpu_custom_call" | custom-call | tf_op jit(solution)/shard_map/grads_reduce/pallas_call | solution.py:579
  209.6 0.0 copy-start.3
  209.6 3.1 %reshape.68 = f32[640,2,256]{2,1,0:T(2,128)} reshape(f32[640,512]{1,0:T(8,128)} %get-tuple-element.18) | data formatting | bytes 2621440 | tf_op jit(solution)/shard_map/reshape | solution.py:624
  212.7 0.0 copy-done.3
  212.7 0.0 copy-start.2
  212.7 1.3 copy.17
  214.0 1.0 copy-done.2
  215.1 0.0 copy-start.1
  215.1 1.3 copy.18
  216.4 1.2 copy-done.1
  217.6 0.0 copy-start
  217.6 1.5 copy.19
  219.1 1.2 copy-done
  220.3 1.5 copy.20
Async XLA Ops:
  209.6 3.1 %copy-start.3 = (bf16[8,64,2048]{2,1,0:T(8,128)(2,1)S(1)}, bf16[8,64,2048]{2,1,0:T(8,128)(2,1)}, u32[]{:S(2)}) copy-start(bf16[8,64,2048]{2,1,0:T(8,128)(2,1)} %get-tuple-element.28) | copy-start | bytes 6291460
  212.7 2.3 %copy-start.2 = (bf16[8,64,2048]{2,1,0:T(8,128)(2,1)S(1)}, bf16[8,64,2048]{2,1,0:T(8,128)(2,1)}, u32[]{:S(2)}) copy-start(bf16[8,64,2048]{2,1,0:T(8,128)(2,1)} %get-tuple-element.29) | copy-start | bytes 6291460
  215.1 2.5 %copy-start.1 = (bf16[512,2560]{1,0:T(8,128)(2,1)S(1)}, bf16[512,2560]{1,0:T(8,128)(2,1)}, u32[]{:S(2)}) copy-start(bf16[512,2560]{1,0:T(8,128)(2,1)} %get-tuple-element.16) | copy-start | bytes 7864324
  217.6 2.7 %copy-start = (bf16[512,2560]{1,0:T(8,128)(2,1)S(1)}, bf16[512,2560]{1,0:T(8,128)(2,1)}, u32[]{:S(2)}) copy-start(bf16[512,2560]{1,0:T(8,128)(2,1)} %get-tuple-element.17) | copy-start | bytes 7864324
